TPU v7x, 512 devices: a whole 4x4x16 slice. The times are simulated.
512 devices in a mesh: seq: 128 (over y_hi, x, z), mp: 4 (over y_lo, core).
Axes of the slice: x: 4, y: 4 (y_hi: 2, y_lo: 2; y = y_hi * 2 + y_lo), z: 16, core: 2. Of those that a mesh axis runs over, the one named last changes fastest.
Arguments:
- queries: bfloat16 [16384, 1200], P('seq', 'mp'), may hold values from -8 to 8
- keys: bfloat16 [16384, 1200], P('seq', 'mp'), may hold values from -8 to 8
- values: bfloat16 [16384, 1200], P('seq', 'mp'), may hold values from -6 to 6
- weight_out: bfloat16 [2560, 1200], P('mp'), may hold values from -0.1875 to 0.1875
- grad_out: bfloat16 [16384, 2560], P('seq', 'mp'), may hold values from -24 to 24
Outputs:
- layer_out: bfloat16 [16384, 2560], P('seq', 'mp')
- grad_queries: bfloat16 [16384, 1200], P('seq', 'mp')
- grad_keys: bfloat16 [16384, 1200], P('seq', 'mp')
- grad_values: bfloat16 [16384, 1200], P('seq', 'mp')
- grad_weight: float32 [2560, 1200], P(('mp', 'seq'))
All inputs are finite; a program needn't handle non-finite values.
Results may differ from a plain program's by a relative error of at most 0.02.
Values may be sent and summed in bfloat16 or wider, within the bound.
A program may use at most 64 MiB of HBM per device.

v0:
```python
import jax
import jax.numpy as jnp
from jax import lax
from jax.sharding import PartitionSpec as P

HD = 150
BLOCK = 1024


NEG = -1e30


def passed_along(block, axis, distance):
    devices = range(lax.axis_size(axis))
    route = [(i - distance, i) for i in devices if i - distance in devices]
    return lax.ppermute(block, axis, route)


def split_heads(array, heads):
    return array.reshape(array.shape[:-1] + (heads, array.shape[-1] // heads))


def body(queries, keys, values, weight_out, grad_out):
    tok = queries.shape[0]
    width = queries.shape[1]
    heads = width // HD
    scale = HD ** (-0.5)
    groups = BLOCK // tok
    nseq = lax.axis_size("seq")
    place = lax.axis_index("seq") % groups
    inner = tok // nseq
    cols = BLOCK // nseq
    rows = tok * nseq // BLOCK
    qhead = split_heads(queries, heads)
    pair = jnp.stack((keys, values))
    pieces = [pair]
    for step in range(1, groups):
        pieces.append(passed_along(pair, "seq", step))
    nearby = jnp.concatenate(pieces, axis=1)
    key_all = split_heads(nearby[0], heads)
    val_all = split_heads(nearby[1], heads)
    qpos = jnp.arange(tok)[:, None]
    kpos = jnp.arange(groups * tok)[None, :]
    source = kpos // tok
    row_mask = (kpos % tok - source * tok <= qpos) & (source <= place)
    row_mask = row_mask[:, None, :]
    row_scores = (
        jnp.einsum("qhd,khd->qhk", qhead, key_all, preferred_element_type=jnp.float32) * scale
    )
    row_max = jnp.max(jnp.where(row_mask, row_scores, NEG), axis=2)
    row_prob = jnp.where(row_mask, jnp.exp(row_scores - row_max[..., None]), 0.0)
    row_total = jnp.sum(row_prob, axis=2)
    row_acc = jnp.einsum(
        "qhk,khd->qhd", row_prob.astype(jnp.bfloat16), val_all, preferred_element_type=jnp.float32
    )
    trio = jnp.stack((queries, keys, values)).reshape(3, inner, nseq, width)
    moved = lax.all_to_all(trio, "seq", split_axis=2, concat_axis=1, tiled=True).reshape(
        3, rows, cols, heads, HD
    )
    col_q, col_k, col_v = (moved[0], moved[1], moved[2])
    col_mask = (jnp.arange(rows)[None, :] < jnp.arange(rows)[:, None])[:, None, None, :]
    col_scores = (
        jnp.einsum("rmhd,smhd->rmhs", col_q, col_k, preferred_element_type=jnp.float32) * scale
    )
    col_max = jnp.max(jnp.where(col_mask, col_scores, NEG), axis=3)
    col_prob = jnp.where(col_mask, jnp.exp(col_scores - col_max[..., None]), 0.0)
    col_total = jnp.sum(col_prob, axis=3)
    col_acc = jnp.einsum(
        "rmhs,smhd->rmhd", col_prob.astype(jnp.bfloat16), col_v, preferred_element_type=jnp.float32
    )
    back = (
        lax.all_to_all(
            col_acc.reshape(1, tok, 1, width), "seq", split_axis=1, concat_axis=2, tiled=True
        ),
        lax.all_to_all(
            col_max.reshape(1, tok, 1, heads), "seq", split_axis=1, concat_axis=2, tiled=True
        ),
        lax.all_to_all(
            col_total.reshape(1, tok, 1, heads), "seq", split_axis=1, concat_axis=2, tiled=True
        ),
    )
    far_acc = back[0].reshape(tok, heads, HD)
    far_max = back[1].reshape(tok, heads)
    far_total = back[2].reshape(tok, heads)
    top = jnp.maximum(row_max, far_max)
    near_w = jnp.exp(row_max - top)
    far_w = jnp.exp(far_max - top)
    total = row_total * near_w + far_total * far_w
    merged = (row_acc * near_w[..., None] + far_acc * far_w[..., None]) / total[..., None]
    attn = merged.reshape(tok, width).astype(jnp.bfloat16)
    lse = top + jnp.log(total)
    attn_full = lax.all_gather(attn, "mp", axis=1, tiled=True)
    layer_out = jnp.einsum(
        "ta,oa->to", attn_full, weight_out, preferred_element_type=jnp.float32
    ).astype(jnp.bfloat16)
    partial_grad = jnp.einsum("to,oa->ta", grad_out, weight_out, preferred_element_type=jnp.float32)
    dattn = lax.psum_scatter(
        partial_grad.astype(jnp.bfloat16), "mp", scatter_dimension=1, tiled=True
    )
    weight_full = jnp.einsum("to,ta->oa", grad_out, attn_full, preferred_element_type=jnp.float32)
    grad_weight = lax.psum_scatter(weight_full, "seq", scatter_dimension=0, tiled=True)
    dhead = split_heads(dattn, heads)
    delta = jnp.sum(
        dhead.astype(jnp.float32) * merged.astype(jnp.bfloat16).astype(jnp.float32), axis=2
    )
    row_p = jnp.where(row_mask, jnp.exp(row_scores - lse[..., None]), 0.0)
    row_dp = jnp.einsum("qhd,khd->qhk", dhead, val_all, preferred_element_type=jnp.float32)
    row_ds = (row_p * (row_dp - delta[..., None])).astype(jnp.bfloat16)
    grad_q = scale * jnp.einsum("qhk,khd->qhd", row_ds, key_all, preferred_element_type=jnp.float32)
    part_k = scale * jnp.einsum("qhk,qhd->khd", row_ds, qhead, preferred_element_type=jnp.float32)
    part_v = jnp.einsum(
        "qhk,qhd->khd", row_p.astype(jnp.bfloat16), dhead, preferred_element_type=jnp.float32
    )
    terms = jnp.stack((part_k, part_v)).reshape(2, groups, tok, width)
    grad_kv = terms[:, 0]
    for step in range(1, groups):
        grad_kv = grad_kv + passed_along(terms[:, step], "seq", -step)
    quad = jnp.stack((queries, keys, values, dattn)).reshape(4, inner, nseq, width)
    fresh = lax.all_to_all(quad, "seq", split_axis=2, concat_axis=1, tiled=True).reshape(
        4, rows, cols, heads, HD
    )
    col_q, col_k, col_v, col_d = (fresh[0], fresh[1], fresh[2], fresh[3])
    info = jnp.stack((lse, delta)).reshape(2, inner, nseq, heads)
    col_info = lax.all_to_all(info, "seq", split_axis=2, concat_axis=1, tiled=True).reshape(
        2, rows, cols, heads
    )
    col_s = jnp.einsum("rmhd,smhd->rmhs", col_q, col_k, preferred_element_type=jnp.float32) * scale
    col_p = jnp.where(col_mask, jnp.exp(col_s - col_info[0][..., None]), 0.0)
    col_dp = jnp.einsum("rmhd,smhd->rmhs", col_d, col_v, preferred_element_type=jnp.float32)
    col_ds = (col_p * (col_dp - col_info[1][..., None])).astype(jnp.bfloat16)
    col_gq = scale * jnp.einsum(
        "rmhs,smhd->rmhd", col_ds, col_k, preferred_element_type=jnp.float32
    )
    col_gk = scale * jnp.einsum(
        "rmhs,rmhd->smhd", col_ds, col_q, preferred_element_type=jnp.float32
    )
    col_gv = jnp.einsum(
        "rmhs,rmhd->smhd", col_p.astype(jnp.bfloat16), col_d, preferred_element_type=jnp.float32
    )
    col_terms = jnp.stack((col_gq, col_gk, col_gv)).reshape(3, tok, 1, width)
    home = (
        lax.all_to_all(
            col_terms.astype(jnp.bfloat16), "seq", split_axis=1, concat_axis=2, tiled=True
        )
        .astype(col_terms.dtype)
        .reshape(3, tok, width)
    )
    grad_queries = (grad_q.reshape(tok, width) + home[0]).astype(jnp.bfloat16)
    grad_keys = (grad_kv[0] + home[1]).astype(jnp.bfloat16)
    grad_values = (grad_kv[1] + home[2]).astype(jnp.bfloat16)
    return (layer_out, grad_queries, grad_keys, grad_values, grad_weight)


def solution(mesh):
    placed = (P("seq", "mp"), P("seq", "mp"), P("seq", "mp"), P("mp", None), P("seq", "mp"))
    return jax.shard_map(
        body,
        mesh=mesh,
        in_specs=placed,
        out_specs=(
            P("seq", "mp"),
            P("seq", "mp"),
            P("seq", "mp"),
            P("seq", "mp"),
            P(("mp", "seq"), None),
        ),
        check_vma=False,
    )
```

profile of v0, /device:TPU:24, one launch (start us, length us, event | category | flops | bytes accessed | tf_op | source)
XLA Modules:
  0.0 1762.1 jit_solution(7094589287668907110)
XLA Ops:
  9.0 11.8 collective-permute-start.5
  20.8 7.8 collective-permute-start.4
  28.6 4.3 collective-permute-start.3
  36.7 17.0 all-to-all-start
  54.4 9.2 fusion
  74.3 27.7 %collective-permute-done = bf16[2,128,300]{1,2,0:T(8,128)(2,1)} collective-permute-done((bf16[2,128,300]{1,2,0:T(8,128)(2,1)S(1)}, bf16[2,128,300]{1,2,0:T(8,128)(2,1)}, u32[]{:S(2)}, u32[]{:S(2)}) %collective-permute-start) | collective-permute-done | bytes 153632 | tf_op jit(solution)/shard_map/ppermute | solution.py:16
  106.6 6.6 collective-permute-start.6
  114.7 3.5 collective-permute-done.2
  123.7 30.8 %all-to-all-start.1 = ((f32[1,128,1,2]{3,2,0,1:T(1,128)}), f32[1,128,1,2]{3,2,0,1:T(1,128)S(1)}, u32[]{:S(2)}, u32[]{:S(2)}) async-start(f32[1,128,1,2]{3,2,0,1:T(1,128)} %bitcast.7), calls=%async_computation.1 | async-start | bytes 131072 | tf_op jit(solution)/shard_map/all_to_all | solution.py:75
  155.3 13.5 all-to-all-done.1
  168.8 8.5 all-to-all-start.3
  178.1 13.8 all-to-all-done.3
  192.5 8.7 all-to-all-start.4
  211.5 9.2 all-to-all-done.4
  220.7 9.8 all-to-all-start.2
  241.0 5.4 all-to-all-done.2
  250.5 13.3 all-to-all-start.5
  263.9 6.2 all-gather
  283.5 6.7 collective-permute-start.7
  290.2 10.1 collective-permute-start.13
  303.5 7.5 all-to-all-start.6
  312.9 12.4 collective-permute-start.12
  325.3 4.2 collective-permute-start.11
  332.0 5.8 collective-permute-start.9
  337.7 6.2 collective-permute-done.13
  343.9 17.5 collective-permute-start.8
  363.0 49.2 %collective-permute-done.12 = f32[2,128,300]{1,2,0:T(8,128)} collective-permute-done((f32[2,128,300]{1,2,0:T(8,128)}, f32[2,128,300]{1,2,0:T(8,128)}, u32[]{:S(2)}, u32[]{:S(2)}) %collective-permute-start.12) | collective-permute-done | bytes 307232 | tf_op jit(solution)/shard_map/ppermute | solution.py:16
  412.2 30.8 %collective-permute-done.11 = f32[2,128,300]{1,2,0:T(8,128)} collective-permute-done((f32[2,128,300]{1,2,0:T(8,128)}, f32[2,128,300]{1,2,0:T(8,128)}, u32[]{:S(2)}, u32[]{:S(2)}) %collective-permute-start.11) | collective-permute-done | bytes 307232 | tf_op jit(solution)/shard_map/ppermute | solution.py:16
  443.0 24.9 %collective-permute-done.10 = f32[2,128,300]{1,2,0:T(8,128)} collective-permute-done((f32[2,128,300]{1,2,0:T(8,128)}, f32[2,128,300]{1,2,0:T(8,128)}, u32[]{:S(2)}, u32[]{:S(2)}) %collective-permute-start.10) | collective-permute-done | bytes 307232 | tf_op jit(solution)/shard_map/ppermute | solution.py:16
  467.9 25.0 %collective-permute-done.9 = f32[2,128,300]{1,2,0:T(8,128)} collective-permute-done((f32[2,128,300]{1,2,0:T(8,128)}, f32[2,128,300]{1,2,0:T(8,128)}, u32[]{:S(2)}, u32[]{:S(2)}) %collective-permute-start.9) | collective-permute-done | bytes 307232 | tf_op jit(solution)/shard_map/ppermute | solution.py:16
  492.9 13.9 collective-permute-done.8
  509.5 1243.4 %all-reduce.5.cloned.1.call-done = f32[640,1200]{0,1:T(8,128)} async-done(((f32[640,1200]{0,1:T(8,128)}), f32[640,1200]{0,1:T(8,128)}) %all-reduce.5.cloned.1.call-update) | async-done | bytes 3072016
  (156 shorter events, 81.4 us)
Async XLA Ops:
  7.2 46.6 %copy-start = (bf16[640,1200]{0,1:T(8,128)(2,1)S(1)}, bf16[640,1200]{0,1:T(8,128)(2,1)}, u32[]{:S(2)}) copy-start(bf16[640,1200]{0,1:T(8,128)(2,1)} %param.8) | copy-start | bytes 4608004
  7.2 46.6 %copy-start.10 = (bf16[128,640]{1,0:T(8,128)(2,1)S(1)}, bf16[128,640]{1,0:T(8,128)(2,1)}, u32[]{:S(2)}) copy-start(bf16[128,640]{1,0:T(8,128)(2,1)} %param.9) | copy-start | bytes 491524
  9.0 168.4 %collective-permute-start.5 = (bf16[2,128,300]{1,2,0:T(8,128)(2,1)S(1)}, bf16[2,128,300]{1,2,0:T(8,128)(2,1)S(1)}, u32[]{:S(2)}, u32[]{:S(2)}) collective-permute-start(bf16[2,128,300]{1,2,0:T(8,128)(2,1)S(1)} %get-tuple-element.53), channel_id=1, source_target_pairs={{0,24},{4,28},{8,32},{12,36},{16,40},{20,44},{24,48},{28,52},{32,5... | collective-permute-start | bytes 460808 | tf_op jit(solution)/shard_map/ppermute | solution.py:16
  20.8 98.9 %collective-permute-start.4 = (bf16[2,128,300]{1,2,0:T(8,128)(2,1)S(1)}, bf16[2,128,300]{1,2,0:T(8,128)(2,1)S(1)}, u32[]{:S(2)}, u32[]{:S(2)}) collective-permute-start(bf16[2,128,300]{1,2,0:T(8,128)(2,1)S(1)} %get-tuple-element.53), channel_id=1, source_target_pairs={{0,20},{4,24},{8,28},{12,32},{16,36},{20,40},{24,44},{28,48},{32,5... | collective-permute-start | bytes 460808 | tf_op jit(solution)/shard_map/ppermute | solution.py:16
  28.6 90.4 %collective-permute-start.3 = (bf16[2,128,300]{1,2,0:T(8,128)(2,1)S(1)}, bf16[2,128,300]{1,2,0:T(8,128)(2,1)S(1)}, u32[]{:S(2)}, u32[]{:S(2)}) collective-permute-start(bf16[2,128,300]{1,2,0:T(8,128)(2,1)S(1)} %get-tuple-element.53), channel_id=1, source_target_pairs={{0,16},{4,20},{8,24},{12,28},{16,32},{20,36},{24,40},{28,44},{32,4... | collective-permute-start | bytes 460808 | tf_op jit(solution)/shard_map/ppermute | solution.py:16
  32.9 73.7 %collective-permute-start.1 = (bf16[2,128,300]{1,2,0:T(8,128)(2,1)S(1)}, bf16[2,128,300]{1,2,0:T(8,128)(2,1)}, u32[]{:S(2)}, u32[]{:S(2)}) collective-permute-start(bf16[2,128,300]{1,2,0:T(8,128)(2,1)S(1)} %get-tuple-element.53), channel_id=1, source_target_pairs={{0,8},{4,12},{8,16},{12,20},{16,24},{20,28},{24,32},{28,36},{32,40... | collective-permute-start | bytes 460808 | tf_op jit(solution)/shard_map/ppermute | solution.py:16
  36.7 83.6 %all-to-all-start = ((bf16[3,1,128,300]{3,0,1,2:T(4,128)(2,1)}), bf16[3,1,128,300]{3,0,1,2:T(4,128)(2,1)S(1)}, u32[]{:S(2)}, u32[]{:S(2)}) async-start(bf16[3,1,128,300]{3,0,1,2:T(4,128)(2,1)} %copy.160), calls=%async_computation | async-start | bytes 786432 | tf_op jit(solution)/shard_map/all_to_all | solution.py:57
  63.6 4.9 collective-permute-start.14
  68.6 33.5 %collective-permute-start = (bf16[2,128,300]{1,2,0:T(8,128)(2,1)S(1)}, bf16[2,128,300]{1,2,0:T(8,128)(2,1)}, u32[]{:S(2)}, u32[]{:S(2)}) collective-permute-start(bf16[2,128,300]{1,2,0:T(8,128)(2,1)S(1)} %get-tuple-element.53), channel_id=1, source_target_pairs={{0,4},{4,8},{8,12},{12,16},{16,20},{20,24},{24,28},{28,32},{32,36}... | collective-permute-start | bytes 460808 | tf_op jit(solution)/shard_map/ppermute | solution.py:16
  102.0 16.2 collective-permute-start.2
  106.6 94.6 %collective-permute-start.6 = (bf16[2,128,300]{1,2,0:T(8,128)(2,1)S(1)}, bf16[2,128,300]{1,2,0:T(8,128)(2,1)S(1)}, u32[]{:S(2)}, u32[]{:S(2)}) collective-permute-start(bf16[2,128,300]{1,2,0:T(8,128)(2,1)S(1)} %get-tuple-element.53), channel_id=1, source_target_pairs={{0,28},{4,32},{8,36},{12,40},{16,44},{20,48},{24,52},{28,56},{32,6... | collective-permute-start | bytes 460808 | tf_op jit(solution)/shard_map/ppermute | solution.py:16
  123.7 45.1 %all-to-all-start.1 = ((f32[1,128,1,2]{3,2,0,1:T(1,128)}), f32[1,128,1,2]{3,2,0,1:T(1,128)S(1)}, u32[]{:S(2)}, u32[]{:S(2)}) async-start(f32[1,128,1,2]{3,2,0,1:T(1,128)} %bitcast.7), calls=%async_computation.1 | async-start | bytes 131072 | tf_op jit(solution)/shard_map/all_to_all | solution.py:75
  168.8 23.0 %all-to-all-start.3 = ((f32[1,128,1,2]{3,2,0,1:T(1,128)}), f32[1,128,1,2]{3,2,0,1:T(1,128)S(1)}, u32[]{:S(2)}, u32[]{:S(2)}) async-start(f32[1,128,1,2]{3,2,0,1:T(1,128)} %bitcast.10), calls=%async_computation.3 | async-start | bytes 131072 | tf_op jit(solution)/shard_map/all_to_all | solution.py:78
  192.5 28.2 %all-to-all-start.4 = ((bf16[4,1,128,300]{3,0,1,2:T(4,128)(2,1)}), bf16[4,1,128,300]{3,0,1,2:T(4,128)(2,1)S(1)}, u32[]{:S(2)}, u32[]{:S(2)}) async-start(bf16[4,1,128,300]{3,0,1,2:T(4,128)(2,1)} %copy.175), calls=%async_computation.4 | async-start | bytes 786432 | tf_op jit(solution)/shard_map/all_to_all | solution.py:119
  211.5 20.8 %copy-start.21 = (f32[128,2]{0,1:T(2,128)}, f32[128,2]{0,1:T(2,128)S(1)}, u32[]{:S(2)}) copy-start(f32[128,2]{0,1:T(2,128)S(1)} %get-tuple-element.37) | copy-start | bytes 3076
  220.7 25.8 %all-to-all-start.2 = ((f32[1,128,1,300]{3,2,0,1:T(1,128)}), f32[1,128,1,300]{3,2,0,1:T(1,128)S(1)}, u32[]{:S(2)}, u32[]{:S(2)}) async-start(f32[1,128,1,300]{3,2,0,1:T(1,128)} %reshape.422), calls=%async_computation.2 | async-start | bytes 393216 | tf_op jit(solution)/shard_map/all_to_all | solution.py:72
  249.7 20.5 %copy-start.17 = (bf16[128,2,150]{0,2,1:T(8,128)(2,1)S(1)}, bf16[128,2,150]{0,2,1:T(8,128)(2,1)}, u32[]{:S(2)}) copy-start(bf16[128,2,150]{0,2,1:T(8,128)(2,1)} %reshape.406) | copy-start | bytes 230404
  250.5 49.8 %all-to-all-start.5 = ((f32[2,1,128,2]{3,0,1,2:T(2,128)}), f32[2,1,128,2]{3,0,1,2:T(2,128)S(1)}, u32[]{:S(2)}, u32[]{:S(2)}) async-start(f32[2,1,128,2]{3,0,1,2:T(2,128)} %bitcast.24), calls=%async_computation.5 | async-start | bytes 262144 | tf_op jit(solution)/shard_map/all_to_all | solution.py:124
  263.9 1489.0 %all-reduce.5.cloned.1.call-start = ((), (), s32[]{:S(2)}) async-start(), calls=%async_computation.7 | async-start | bytes 6144000
  280.5 20.2 %copy-start.14 = (bf16[16,8,2,150]{3,2,1,0:T(2,128)(2,1)S(1)}, bf16[16,8,2,150]{3,2,1,0:T(2,128)(2,1)}, u32[]{:S(2)}) copy-start(bf16[16,8,2,150]{3,2,1,0:T(2,128)(2,1)} %squeeze.63) | copy-start | bytes 230404
  280.5 20.2 %copy-start.15 = (bf16[16,8,2,150]{3,2,1,0:T(2,128)(2,1)S(1)}, bf16[16,8,2,150]{3,2,1,0:T(2,128)(2,1)}, u32[]{:S(2)}) copy-start(bf16[16,8,2,150]{3,2,1,0:T(2,128)(2,1)} %squeeze.64) | copy-start | bytes 230404
  280.5 20.4 %copy-start.13 = (bf16[16,8,2,150]{3,2,1,0:T(2,128)(2,1)S(1)}, bf16[16,8,2,150]{3,2,1,0:T(2,128)(2,1)}, u32[]{:S(2)}) copy-start(bf16[16,8,2,150]{3,2,1,0:T(2,128)(2,1)} %squeeze.65) | copy-start | bytes 230404
  283.5 48.5 %collective-permute-start.7 = (f32[2,128,300]{1,2,0:T(8,128)}, f32[2,128,300]{1,2,0:T(8,128)}, u32[]{:S(2)}, u32[]{:S(2)}) collective-permute-start(f32[2,128,300]{1,2,0:T(8,128)} %get-tuple-element.41), channel_id=1, source_target_pairs={{4,0},{8,4},{12,8},{16,12},{20,16},{24,20},{28,24},{32,28},{36,32}... | collective-permute-start | bytes 921608 | tf_op jit(solution)/shard_map/ppermute | solution.py:16
  290.2 53.7 %collective-permute-start.13 = (f32[2,128,300]{1,2,0:T(8,128)}, f32[2,128,300]{1,2,0:T(8,128)}, u32[]{:S(2)}, u32[]{:S(2)}) collective-permute-start(f32[2,128,300]{1,2,0:T(8,128)} %get-tuple-element.42), channel_id=1, source_target_pairs={{28,0},{32,4},{36,8},{40,12},{44,16},{48,20},{52,24},{56,28},{60,3... | collective-permute-start | bytes 921608 | tf_op jit(solution)/shard_map/ppermute | solution.py:16
  302.2 59.3 %copy-start.5 = (bf16[1024,2,150]{0,2,1:T(8,128)(2,1)S(1)}, bf16[1024,2,150]{0,2,1:T(8,128)(2,1)}, u32[]{:S(2)}) copy-start(bf16[1024,2,150]{0,2,1:T(8,128)(2,1)} %copy-done.4) | copy-start | bytes 1843204
  302.2 59.3 %copy-start.6 = (bf16[128,2,1024]{0,2,1:T(8,128)(2,1)S(1)}, bf16[128,2,1024]{0,2,1:T(8,128)(2,1)}, u32[]{:S(2)}) copy-start(bf16[128,2,1024]{0,2,1:T(8,128)(2,1)} %fusion.5) | copy-start | bytes 1572868
  303.5 205.0 %all-to-all-start.6 = ((bf16[3,128,1,300]{3,0,2,1:T(4,128)(2,1)}), bf16[3,128,1,300]{3,0,2,1:T(4,128)(2,1)S(1)}, u32[]{:S(2)}, u32[]{:S(2)}) async-start(bf16[3,128,1,300]{3,0,2,1:T(4,128)(2,1)} %copy.194), calls=%async_computation.6 | async-start | bytes 786432 | tf_op jit(solution)/shard_map/all_to_all | solution.py:142
  312.9 99.3 %collective-permute-start.12 = (f32[2,128,300]{1,2,0:T(8,128)}, f32[2,128,300]{1,2,0:T(8,128)}, u32[]{:S(2)}, u32[]{:S(2)}) collective-permute-start(f32[2,128,300]{1,2,0:T(8,128)} %get-tuple-element.43), channel_id=1, source_target_pairs={{24,0},{28,4},{32,8},{36,12},{40,16},{44,20},{48,24},{52,28},{56,3... | collective-permute-start | bytes 921608 | tf_op jit(solution)/shard_map/ppermute | solution.py:16
  325.3 117.7 %collective-permute-start.11 = (f32[2,128,300]{1,2,0:T(8,128)}, f32[2,128,300]{1,2,0:T(8,128)}, u32[]{:S(2)}, u32[]{:S(2)}) collective-permute-start(f32[2,128,300]{1,2,0:T(8,128)} %get-tuple-element.44), channel_id=1, source_target_pairs={{20,0},{24,4},{28,8},{32,12},{36,16},{40,20},{44,24},{48,28},{52,3... | collective-permute-start | bytes 921608 | tf_op jit(solution)/shard_map/ppermute | solution.py:16
  329.5 138.4 %collective-permute-start.10 = (f32[2,128,300]{1,2,0:T(8,128)}, f32[2,128,300]{1,2,0:T(8,128)}, u32[]{:S(2)}, u32[]{:S(2)}) collective-permute-start(f32[2,128,300]{1,2,0:T(8,128)} %get-tuple-element.45), channel_id=1, source_target_pairs={{16,0},{20,4},{24,8},{28,12},{32,16},{36,20},{40,24},{44,28},{48,3... | collective-permute-start | bytes 921608 | tf_op jit(solution)/shard_map/ppermute | solution.py:16
  332.0 160.9 %collective-permute-start.9 = (f32[2,128,300]{1,2,0:T(8,128)}, f32[2,128,300]{1,2,0:T(8,128)}, u32[]{:S(2)}, u32[]{:S(2)}) collective-permute-start(f32[2,128,300]{1,2,0:T(8,128)} %get-tuple-element.46), channel_id=1, source_target_pairs={{12,0},{16,4},{20,8},{24,12},{28,16},{32,20},{36,24},{40,28},{44,3... | collective-permute-start | bytes 921608 | tf_op jit(solution)/shard_map/ppermute | solution.py:16
  343.9 162.8 %collective-permute-start.8 = (f32[2,128,300]{1,2,0:T(8,128)}, f32[2,128,300]{1,2,0:T(8,128)}, u32[]{:S(2)}, u32[]{:S(2)}) collective-permute-start(f32[2,128,300]{1,2,0:T(8,128)} %get-tuple-element.47), channel_id=1, source_target_pairs={{8,0},{12,4},{16,8},{20,12},{24,16},{28,20},{32,24},{36,28},{40,32... | collective-permute-start | bytes 921608 | tf_op jit(solution)/shard_map/ppermute | solution.py:16
  (15 other events, 89.5 us)
Sparse Core Ops, SparseCore 0:
  278.1 1474.8 all-reduce.4
where the time goes:
time: 1760 us
  waiting for transfers between devices  1470 us (84%)
  starting transfers between devices  195 us (11%)
  local copies, waits for them, and re-layouts  47.7 us (3%)
    unnamed x3, waiting for transfers between devices  1240 us
    ppermute x14, waiting for transfers between devices, passed_along(): return lax.ppermute(block, axis, route)  181 us
    ppermute x14, starting transfers between devices, passed_along(): return lax.ppermute(block, axis, route)  97.9 us
  transfers between devices with their start and end apart: 23, of which 13 were waited for; matrix products, arithmetic and copies ran while one was open for 4% of the time, Pallas kernels for 0%

commit v1 on v0

v1 whole, which is shorter than its diff:
```python
import jax
import jax.numpy as jnp
from jax import lax
from jax.experimental import pallas as pl
from jax.experimental.pallas import tpu as pltpu
from jax.sharding import PartitionSpec as P

MESH = pl.DeviceIdType.MESH
HD = 150
W = 300
WP = 384
TOK = 128
NEG = -1e30
SCALE = HD ** (-0.5)
F32 = jnp.float32
BF16 = jnp.bfloat16


def nn(a, b):
    return jnp.dot(a, b, preferred_element_type=F32)


def nt(a, b):
    return lax.dot_general(a, b, (((1,), (1,)), ((), ())), preferred_element_type=F32)


def tn(a, b):
    return lax.dot_general(a, b, (((0,), (0,)), ((), ())), preferred_element_type=F32)


def iota(shape, dim):
    return lax.broadcasted_iota(jnp.int32, shape, dim)


def head_pair(x):
    lane = iota(x.shape, 1)
    a = jnp.where(lane < HD, x, 0.0)
    b = jnp.where((lane >= HD) & (lane < W), x, 0.0)
    return jnp.concatenate([a, b], axis=0).astype(BF16)


def pick(x2):
    n = x2.shape[0] // 2
    lane = iota((n, WP), 1)
    return jnp.where(lane < HD, x2[:n], x2[n:])


def padded(x):
    x = x.astype(F32)
    return jnp.concatenate([x, jnp.zeros((x.shape[0], WP - x.shape[1]), F32)], axis=1)


def kernel(
    q_ref, k_ref, v_ref, w_ref, go_ref,
    lay_ref, gq_ref, gk_ref, gv_ref, gw_ref,
    kv, q2, d2, acc2, m_ref, l_ref, gq2, own,
    part, mpin, colx, colin, cold, coldin, colo, coloin, coli, coliin, colg, colgin,
    att, goh, goin, gwin, gz1, z1in, gz2, z2in, gfx, fxin, rbs, rbin, info_t, dat,
    row_s, row_r, rb_s, rb_r, mp_s, mp_r, ag_s, ag_r,
    ca_s, ca_r, cd_s, cd_r, co_s, co_r, ci_s, ci_r, cg_s, cg_r,
    go_s, go_r, gw_s, gw_r, z1_s, z1_r, z2_s, z2_r, fx_s, fx_r,
):
    s = lax.axis_index("seq")
    m = lax.axis_index("mp")
    r, cg = s // 8, s % 8
    yh, x, z = s // 64, (s // 16) % 4, s % 16
    zq, zr = z // 4, z % 4
    g = yh * 4 + x

    def copy(src, dst, ss, rs, dev):
        return pltpu.make_async_remote_copy(
            src_ref=src, dst_ref=dst, send_sem=ss, recv_sem=rs, device_id=dev, device_id_type=MESH
        )

    def col_dev(rr):
        return (rr * 8 + cg, m)

    def g_dev(gg):
        return ((gg // 4) * 64 + (gg % 4) * 16 + z, m)

    def z_dev(zz):
        return (yh * 64 + x * 16 + zz, m)

    def x_dev(xx):
        return (yh * 64 + xx * 16 + z, m)

    bar = pltpu.get_barrier_semaphore()

    def greet(dev):
        pl.semaphore_signal(bar, inc=1, device_id=dev, device_id_type=MESH)

    def each(n, f):
        lax.fori_loop(1, n, lambda i, c: (f(i), c)[1], 0)

    each(16, lambda i: greet(col_dev((r + i) % 16)))
    each(4, lambda i: greet((s, (m + i) % 4)))
    each(4, lambda i: greet(z_dev(zq * 4 + (zr + i) % 4)))
    each(4, lambda i: greet(z_dev(((zq + i) % 4) * 4 + zr)))

    @pl.when(cg > 0)
    def _():
        greet((s - 1, m))

    @pl.when(cg < 7)
    def _():
        greet((s + 1, m))

    q32 = padded(q_ref[...])
    k32 = padded(k_ref[...])
    v32 = padded(v_ref[...])
    kv[0, 0] = k32.astype(BF16)
    kv[0, 1] = v32.astype(BF16)
    q2[...] = head_pair(q32)
    blocks = [t.reshape(16, 8, WP) for t in (q32, k32, v32, jnp.zeros_like(q32))]
    colx[...] = jnp.concatenate(blocks, axis=1).astype(BF16)
    pg = nn(go_ref[...], w_ref[...])
    for i in range(4):
        part[i] = padded(pg[:, W * i : W * i + W]).astype(BF16)
    go32 = go_ref[...].astype(F32)
    zer = jnp.zeros((TOK, WP - 320), F32)
    goh[0] = jnp.concatenate([go32[:, :320], zer], axis=1).astype(BF16)
    goh[1] = jnp.concatenate([go32[:, 320:], zer], axis=1).astype(BF16)

    links = (cg > 0).astype(jnp.int32) + (cg < 7).astype(jnp.int32)
    pl.semaphore_wait(bar, 15 + 3 + 3 + 3 + links)

    def row_copy(t, i):
        return copy(kv.at[t, i], kv.at[t + 1, i], row_s.at[t, i], row_r.at[t + 1, i], (s + 1, m))

    def row_send(t):
        @pl.when(cg < 7)
        def _():
            row_copy(t, 0).start()
            row_copy(t, 1).start()

    row_send(0)

    def mp_copy(i):
        o = (m + i) % 4
        return copy(part.at[o], mpin.at[m], mp_s.at[o], mp_r.at[m], (s, o))

    each(4, lambda i: mp_copy(i).start())

    def col_send(src, dst, ss, rs, i):
        o = (r + i) % 16
        return copy(src.at[o], dst.at[r], ss.at[o], rs.at[r], col_dev(o))

    def col_wait(src, dst, ss, rs, i):
        o = (r + i) % 16
        copy(src.at[o], dst.at[o], ss.at[o], rs.at[o], col_dev(o)).wait_recv()

    each(16, lambda i: col_send(colx, colin, ca_s, ca_r, i).start())
    colin[r] = colx[r]

    def go_copy(i):
        o = (g + i) % 8
        return copy(goh.at[o // 4], goin.at[g], go_s.at[o], go_r.at[g], g_dev(o))

    each(8, lambda i: go_copy(i).start())
    goin[g] = goh[yh]

    def scores(t):
        return nt(q2[...], kv[t, 0]) * SCALE

    def row_first():
        sc = scores(0)
        ok = iota((256, TOK), 0) % TOK >= iota((256, TOK), 1)
        sc = jnp.where(ok, sc, NEG)
        mx = jnp.max(sc, axis=1, keepdims=True)
        p = jnp.exp(sc - mx)
        m_ref[...] = mx
        l_ref[...] = jnp.sum(p, axis=1, keepdims=True)
        acc2[...] = nn(p.astype(BF16), kv[0, 1])

    def row_step(t):
        @pl.when(cg >= t)
        def _():
            for i in range(2):
                copy(kv.at[t, i], kv.at[t, i], row_s.at[t, i], row_r.at[t, i], (s - 1, m)).wait_recv()

                @pl.when(cg < 7)
                def _():
                    row_copy(t, i).start()

            sc = scores(t)
            old = m_ref[...]
            mx = jnp.maximum(old, jnp.max(sc, axis=1, keepdims=True))
            p = jnp.exp(sc - mx)
            w = jnp.exp(old - mx)
            m_ref[...] = mx
            l_ref[...] = l_ref[...] * w + jnp.sum(p, axis=1, keepdims=True)
            acc2[...] = acc2[...] * w + nn(p.astype(BF16), kv[t, 1])

    row_first()

    def finish_dattn():
        d = part[m].astype(F32)
        for i in range(1, 4):
            o = (m + i) % 4
            copy(part.at[o], mpin.at[o], mp_s.at[o], mp_r.at[o], (s, o)).wait_recv()
            d = d + mpin[o].astype(F32)
        d = d.astype(BF16).astype(F32)
        dat[...] = d
        d2[...] = head_pair(d)
        cold[...] = d.reshape(16, 8, WP)
        each(16, lambda i: col_send(cold, coldin, cd_s, cd_r, i).start())
        coldin[r] = cold[r]

    finish_dattn()
    lax.fori_loop(1, 5, lambda t, c: (row_step(t), c)[1], 0)

    def col_part(i):
        c = colin[...].astype(F32)
        return c[:, 8 * i : 8 * i + 8, :].reshape(TOK, WP)

    def col_forward():
        each(16, lambda i: col_wait(colx, colin, ca_s, ca_r, i))
        cq2 = head_pair(col_part(0))
        ck = col_part(1).astype(BF16)
        cv = col_part(2).astype(BF16)
        sc = nt(cq2, ck) * SCALE
        qi = iota((256, TOK), 0) % TOK
        ki = iota((256, TOK), 1)
        ok = (qi % 8 == ki % 8) & (ki // 8 < qi // 8)
        mx = jnp.max(jnp.where(ok, sc, NEG), axis=1, keepdims=True)
        p = jnp.where(ok, jnp.exp(sc - mx), 0.0)
        tot = jnp.sum(p, axis=1, keepdims=True)
        some = tot > 0.0
        safe = jnp.where(some, tot, 1.0)
        o = pick(nn(p.astype(BF16), cv) / safe)
        lse = jnp.where(some, mx + jnp.log(safe), NEG)
        lane = iota((TOK, WP), 1)
        o = jnp.where(lane < W, o, jnp.where(lane < 340, lse[:TOK], lse[TOK:]))
        colo[...] = o.reshape(16, 8, WP)
        each(16, lambda i: col_send(colo, coloin, co_s, co_r, i).start())
        coloin[r] = colo[r]

    col_forward()
    lax.fori_loop(5, 8, lambda t, c: (row_step(t), c)[1], 0)

    def ag_copy(i):
        o = (m + i) % 4
        return copy(att.at[m], att.at[m], ag_s.at[o], ag_r.at[m], (s, o))

    def merge():
        each(16, lambda i: col_wait(colo, coloin, co_s, co_r, i))
        far = coloin[...].reshape(TOK, WP)
        lane = iota((TOK, WP), 1)
        d = dat[...]
        near = pick(acc2[...])
        lses, near_w, far_w = [], [], []
        for h in range(2):
            lo = W + 40 * h
            here = (lane >= lo) & (lane < lo + 40)
            fl = jnp.max(jnp.where(here, far, -3e38), axis=1, keepdims=True)
            mr = m_ref[h * TOK : h * TOK + TOK, :]
            nl = mr + jnp.log(l_ref[h * TOK : h * TOK + TOK, :])
            top = jnp.maximum(nl, fl)
            lse = top + jnp.log(jnp.exp(nl - top) + jnp.exp(fl - top))
            lses.append(lse)
            near_w.append(jnp.exp(mr - lse))
            far_w.append(jnp.exp(fl - lse))
        nw = jnp.where(lane < HD, near_w[0], near_w[1])
        fw = jnp.where(lane < HD, far_w[0], far_w[1])
        a = jnp.where(lane < W, near * nw + far * fw, 0.0).astype(BF16)
        att[m] = a
        each(4, lambda i: ag_copy(i).start())
        prod = a.astype(F32) * d
        d0 = jnp.sum(jnp.where(lane < HD, prod, 0.0), axis=1, keepdims=True)
        d1 = jnp.sum(jnp.where((lane >= HD) & (lane < W), prod, 0.0), axis=1, keepdims=True)
        ln = iota((TOK, TOK), 1)
        info = jnp.where(ln < 64, jnp.where(ln < 32, lses[0], lses[1]), jnp.where(ln < 96, d0, d1))
        coli[...] = info.reshape(16, 8, TOK)
        each(16, lambda i: col_send(coli, coliin, ci_s, ci_r, i).start())
        coliin[r] = coli[r]
        info_t[...] = info.T
        gq2[...] = jnp.zeros_like(gq2)

    merge()

    def stats(it):
        lse = jnp.concatenate([it[0:1], it[32:33]], axis=1)
        delta = jnp.concatenate([it[64:65], it[96:97]], axis=1)
        return lse, delta

    def row_own(u):
        @pl.when(cg >= u)
        def _():
            t = cg - u
            lse, delta = stats(info_t[...])
            k_t, v_t = kv[t, 0], kv[t, 1]
            sc = nt(k_t, q2[...]) * SCALE
            ok = (t > 0) | (iota((TOK, 256), 0) <= iota((TOK, 256), 1) % TOK)
            p = jnp.where(ok, jnp.exp(sc - lse), 0.0)
            dp = nt(v_t, d2[...])
            ds = (p * (dp - delta)).astype(BF16)
            own[u, 0] = nn(ds, q2[...]) * SCALE
            own[u, 1] = nn(p.astype(BF16), d2[...])
            gq2[...] += tn(ds, k_t)

    def rb_copy(u, i):
        return copy(rbs.at[u, i], rbin.at[u, i], rb_s.at[u, i], rb_r.at[u, i], (s - 1, m))

    def row_chain(u):
        @pl.when(cg >= u)
        def _():
            for i in range(2):
                @pl.when(cg < 7)
                def _():
                    rb_copy(u, i).wait_recv()
                    own[u, i] += rbin[u, i].astype(F32)

                @pl.when(cg > u)
                def _():
                    rbs[u, i] = own[u, i].astype(BF16)
                    rb_copy(u, i).start()

    def gw_copy(i):
        o = (g + i) % 8
        return copy(att.at[o % 4], gwin.at[g], gw_s.at[o], gw_r.at[g], g_dev(o))

    def gather_attn():
        for i in range(1, 4):
            o = (m + i) % 4
            copy(att.at[o], att.at[o], ag_s.at[o], ag_r.at[o], (s, o)).wait_recv()
        each(8, lambda i: gw_copy(i).start())
        gwin[g] = att[x]

    def layer():
        full = jnp.concatenate([att[i].astype(F32)[:, :W] for i in range(4)], axis=1).astype(BF16)
        lay_ref[...] = nt(full, w_ref[...]).astype(BF16)

    def z1_copy(i):
        o = (zr + i) % 4
        return copy(gz1.at[o], z1in.at[zr], z1_s.at[o], z1_r.at[zr], z_dev(zq * 4 + o))

    def gw_product():
        def arrived(i):
            o = (g + i) % 8
            copy(goh.at[0], goin.at[o], go_s.at[o], go_r.at[o], g_dev(o)).wait_recv()
            copy(att.at[0], gwin.at[o], gw_s.at[o], gw_r.at[o], g_dev(o)).wait_recv()

        each(8, arrived)
        prod = tn(goin[...].reshape(8 * TOK, WP), gwin[...].reshape(8 * TOK, WP)).astype(BF16)
        to = iota((512, WP), 0)
        i5 = to % 8
        xx = (to // 8) % 4
        qq = (to // 32) % 4
        rr = to // 128
        src = jnp.where(i5 < 5, (xx * 16 + qq * 4 + rr) * 5 + i5, -1)
        perm = (src == iota((512, WP), 1)).astype(F32).astype(BF16)
        gz1[...] = nn(perm, prod).astype(BF16).reshape(4, TOK, WP)
        each(4, lambda i: z1_copy(i).start())

    def z2_copy(i):
        o = (zq + i) % 4
        return copy(gz2.at[o], z2in.at[zq], z2_s.at[o], z2_r.at[zq], z_dev(o * 4 + zr))

    def gw_level1():
        t = gz1[zr].astype(F32)
        for i in range(1, 4):
            o = (zr + i) % 4
            copy(gz1.at[o], z1in.at[o], z1_s.at[o], z1_r.at[o], z_dev(zq * 4 + o)).wait_recv()
            t = t + z1in[o].astype(F32)
        gz2[...] = t.astype(BF16).reshape(4, 32, WP)
        each(4, lambda i: z2_copy(i).start())

    def fx_copy(i):
        o = (x + i) % 4
        return copy(gfx.at[o], fxin.at[x], fx_s.at[o], fx_r.at[x], x_dev(o))

    def gw_level2():
        t = gz2[zq].astype(F32)
        for i in range(1, 4):
            o = (zq + i) % 4
            copy(gz2.at[o], z2in.at[o], z2_s.at[o], z2_r.at[o], z_dev(o * 4 + zr)).wait_recv()
            t = t + z2in[o].astype(F32)
        gfx[...] = t.reshape(4, 8, WP)
        each(4, lambda i: fx_copy(i).start())
        fxin[x] = gfx[x]

    def gw_finish():
        for i in range(1, 4):
            o = (x + i) % 4
            copy(gfx.at[o], fxin.at[o], fx_s.at[o], fx_r.at[o], x_dev(o)).wait_recv()
        gw_ref[...] = jnp.concatenate([fxin[i][:, :W] for i in range(4)], axis=1)[:5]

    def col_backward():
        each(16, lambda i: col_wait(cold, coldin, cd_s, cd_r, i))
        each(16, lambda i: col_wait(coli, coliin, ci_s, ci_r, i))
        cq2 = head_pair(col_part(0))
        ck = col_part(1).astype(BF16)
        cv = col_part(2).astype(BF16)
        cd2 = head_pair(coldin[...].reshape(TOK, WP))
        lse, delta = stats(coliin[...].reshape(TOK, TOK).T)
        sc = nt(ck, cq2) * SCALE
        ki = iota((TOK, 256), 0)
        qi = iota((TOK, 256), 1) % TOK
        ok = (qi % 8 == ki % 8) & (ki // 8 < qi // 8)
        p = jnp.where(ok, jnp.exp(sc - lse), 0.0)
        dp = nt(cv, cd2)
        ds = (p * (dp - delta)).astype(BF16)
        ggk = nn(ds, cq2) * SCALE
        ggv = nn(p.astype(BF16), cd2)
        ggq = pick(tn(ds, ck)) * SCALE
        out = [t.reshape(16, 8, WP) for t in (ggq, ggk, ggv, jnp.zeros_like(ggq))]
        colg[...] = jnp.concatenate(out, axis=1).astype(BF16)
        each(16, lambda i: col_send(colg, colgin, cg_s, cg_r, i).start())
        colgin[r] = colg[r]

    row_own(0)

    @pl.when(cg == 7)
    def _():
        row_chain(0)

    gather_attn()

    @pl.when(cg < 4)
    def _():
        col_backward()
        gw_product()

    layer()

    @pl.when(cg < 7)
    def _():
        row_chain(0)

    def both(u):
        row_own(u)
        row_chain(u)

    lax.fori_loop(1, 3, lambda u, c: (both(u), c)[1], 0)

    @pl.when(cg >= 4)
    def _():
        col_backward()
        gw_product()

    lax.fori_loop(3, 8, lambda u, c: (both(u), c)[1], 0)
    gw_level1()
    gw_level2()

    each(16, lambda i: col_wait(colg, colgin, cg_s, cg_r, i))
    home = colgin[...].astype(F32)
    hq, hk, hv = (home[:, 8 * i : 8 * i + 8, :].reshape(TOK, WP) for i in range(3))
    gq_ref[...] = (pick(gq2[...]) * SCALE + hq)[:, :W].astype(BF16)
    gk_ref[...] = (own[cg, 0] + hk)[:, :W].astype(BF16)
    gv_ref[...] = (own[cg, 1] + hv)[:, :W].astype(BF16)
    gw_finish()

    def sent(t, c):
        @pl.when((cg < 7) & (t <= cg))
        def _():
            row_copy(t, 0).wait_send()
            row_copy(t, 1).wait_send()

        @pl.when(t < cg)
        def _():
            rb_copy(t, 0).wait_send()
            rb_copy(t, 1).wait_send()

        return c

    lax.fori_loop(0, 8, sent, 0)
    for f in (mp_copy, ag_copy, z1_copy, z2_copy, fx_copy):
        each(4, lambda i, f=f: f(i).wait_send())
    for f in (go_copy, gw_copy):
        each(8, lambda i, f=f: f(i).wait_send())

    def col_sent(i):
        col_send(colx, colin, ca_s, ca_r, i).wait_send()
        col_send(cold, coldin, cd_s, cd_r, i).wait_send()
        col_send(colo, coloin, co_s, co_r, i).wait_send()
        col_send(coli, coliin, ci_s, ci_r, i).wait_send()
        col_send(colg, colgin, cg_s, cg_r, i).wait_send()

    each(16, col_sent)


def body(queries, keys, values, weight_out, grad_out):
    vm = pl.BlockSpec(memory_space=pltpu.VMEM)
    dma = pltpu.SemaphoreType.DMA
    vmem = pltpu.VMEM
    out = jax.ShapeDtypeStruct
    scratch = [
        vmem((8, 2, TOK, WP), BF16),
        vmem((256, WP), BF16),
        vmem((256, WP), BF16),
        vmem((256, WP), F32),
        vmem((256, 1), F32),
        vmem((256, 1), F32),
        vmem((256, WP), F32),
        vmem((8, 2, TOK, WP), F32),
        vmem((4, TOK, WP), BF16),
        vmem((4, TOK, WP), BF16),
        vmem((16, 32, WP), BF16),
        vmem((16, 32, WP), BF16),
        vmem((16, 8, WP), F32),
        vmem((16, 8, WP), F32),
        vmem((16, 8, WP), F32),
        vmem((16, 8, WP), F32),
        vmem((16, 8, TOK), F32),
        vmem((16, 8, TOK), F32),
        vmem((16, 32, WP), BF16),
        vmem((16, 32, WP), BF16),
        vmem((4, TOK, WP), BF16),
        vmem((2, TOK, WP), BF16),
        vmem((8, TOK, WP), BF16),
        vmem((8, TOK, WP), BF16),
        vmem((4, TOK, WP), BF16),
        vmem((4, TOK, WP), BF16),
        vmem((4, 32, WP), BF16),
        vmem((4, 32, WP), BF16),
        vmem((4, 8, WP), F32),
        vmem((4, 8, WP), F32),
        vmem((8, 2, TOK, WP), BF16),
        vmem((8, 2, TOK, WP), BF16),
        vmem((TOK, TOK), F32),
        vmem((TOK, WP), F32),
    ]
    sems = [dma((8, 2))] * 4 + [dma((4,))] * 4 + [dma((16,))] * 10 + [dma((8,))] * 4 + [dma((4,))] * 6
    return pl.pallas_call(
        kernel,
        out_shape=(
            out((TOK, 640), BF16),
            out((TOK, W), BF16),
            out((TOK, W), BF16),
            out((TOK, W), BF16),
            out((5, 4 * W), F32),
        ),
        in_specs=[vm] * 5,
        out_specs=[vm] * 5,
        scratch_shapes=scratch + sems,
        compiler_params=pltpu.CompilerParams(
            collective_id=0, has_side_effects=True, vmem_limit_bytes=50 * 2**20
        ),
    )(queries, keys, values, weight_out, grad_out)


def solution(mesh):
    placed = (P("seq", "mp"), P("seq", "mp"), P("seq", "mp"), P("mp", None), P("seq", "mp"))
    return jax.shard_map(
        body,
        mesh=mesh,
        in_specs=placed,
        out_specs=(
            P("seq", "mp"),
            P("seq", "mp"),
            P("seq", "mp"),
            P("seq", "mp"),
            P(("mp", "seq"), None),
        ),
        check_vma=False,
    )
```

time: 1760 us -> 172 us (0.10)
  waiting for transfers between devices: 1470 us -> 0 us
  starting transfers between devices: 195 us -> 0 us
  Pallas kernels: 0 us -> 159 us
  local copies, waits for them, and re-layouts: 47.7 us -> 9.24 us
    unnamed x3 -> x0, waiting for transfers between devices: 1240 us -> none
    ppermute x14 -> x0, waiting for transfers between devices: 181 us -> none  [passed_along(): return lax.ppermute(block, axis, route)]
    pallas_call x0 -> x1, Pallas kernels: none -> 159 us  [body(): pl.pallas_call(kernel, out_shape=(out((TOK, 640), BF16), out((TOK, W), BF...]
    ppermute x14 -> x0, starting transfers between devices: 97.9 us -> none  [passed_along(): return lax.ppermute(block, axis, route)]
    all_to_all x7 -> x0, starting transfers between devices: 95.6 us -> none  [the longest x1 30.8 us: body(): lax.all_to_all(col_max.reshape(1, tok, 1, heads), 'seq', split_axis=1, co...]
    all_to_all x7 -> x0, waiting for transfers between devices: 41.9 us -> none  [the longest x1 13.8 us: body(): lax.all_to_all(col_total.reshape(1, tok, 1, heads), 'seq', split_axis=1,...]
  transfers between devices with their start and end apart: 23 -> 0, of which waited for: 13 -> 0; matrix products, arithmetic and copies ran while one was open for 4% -> 0% of each run, Pallas kernels for 0% -> 0%
where the time goes in v1:
time: 172 us; the launch traced here: 169 us
  Pallas kernels  159 us (92%)
  local copies, waits for them, and re-layouts  9.24 us (5%)
    pallas_call x1, Pallas kernels, body(): pl.pallas_call(kernel, out_shape=(out((TOK, 640), BF16), out((TOK, W), BF...  159 us
    unnamed x8, local copies, waits for them, and re-layouts  7.01 us

profile of v1, /device:TPU:24, one launch (start us, length us, event | category | flops | bytes accessed | tf_op | source)
XLA Modules:
  0.0 168.7 jit_solution(2725855252479447557)
XLA Ops:
  0.6 1.0 copy.10.q_ref
  1.6 1.0 copy.11.k_ref
  2.6 0.0 copy-start
  2.7 1.0 copy.12.v_ref
  3.7 2.7 %copy.13.w_ref = bf16[640,1200]{1,0:T(8,128)(2,1)S(1)} copy(bf16[640,1200]{0,1:T(8,128)(2,1)} %param.8) | data formatting | bytes 3072000 | tf_op args[3]
  6.4 0.0 copy-done
  6.4 158.8 %shard_map.92 = (bf16[128,640]{1,0:T(8,128)(2,1)S(1)}, bf16[128,300]{1,0:T(8,128)(2,1)S(1)}, bf16[128,300]{1,0:T(8,128)(2,1)S(1)}, bf16[128,300]{1,0:T(8,128)(2,1)S(1)}, f32[5,1200]{1,0:T(8,128)S(1)}) custom-call(bf16[128,300]{1,0:T(8,128)(2,1)S(1)} %copy.10.q_ref, bf16[128,300]{1,0:T(8,128)(2,1)S(1)} %copy.11.k_ref, bf16[128,300]{1,0:T(8,128)(2,1)S(1)} %copy.12.v_ref, ...), custom_call_target="tpu_custom_call" | custom-call | tf_op jit(solution)/shard_map/pallas_call | solution.py:524
  165.2 0.7 copy.14
  166.0 0.7 copy.15
  166.7 0.7 copy.16
  167.5 0.7 copy.19
  168.1 0.6 copy.20
Async XLA Ops:
  2.6 3.7 %copy-start = (bf16[128,640]{1,0:T(8,128)(2,1)S(1)}, bf16[128,640]{1,0:T(8,128)(2,1)}, u32[]{:S(2)}) copy-start(bf16[128,640]{1,0:T(8,128)(2,1)} %go_ref.1) | copy-start | bytes 491524

commit v2 on v1

v2 whole, which is shorter than its diff:
```python
import jax
import jax.numpy as jnp
from jax import lax
from jax.experimental import pallas as pl
from jax.experimental.pallas import tpu as pltpu
from jax.sharding import PartitionSpec as P

MESH = pl.DeviceIdType.MESH
HD = 150
W = 300
WP = 384
WR = 304
TOK = 128
NEG = -1e30
SCALE = HD ** (-0.5)
F32 = jnp.float32
BF16 = jnp.bfloat16


def nn(a, b):
    return jnp.dot(a, b, preferred_element_type=F32)


def nt(a, b):
    return lax.dot_general(a, b, (((1,), (1,)), ((), ())), preferred_element_type=F32)


def tn(a, b):
    return lax.dot_general(a, b, (((0,), (0,)), ((), ())), preferred_element_type=F32)


def iota(shape, dim):
    return lax.broadcasted_iota(jnp.int32, shape, dim)


def head_pair(x):
    lane = iota(x.shape, 1)
    a = jnp.where(lane < HD, x, 0.0)
    b = jnp.where((lane >= HD) & (lane < W), x, 0.0)
    return jnp.concatenate([a, b], axis=0).astype(BF16)


def head_columns(x):
    row = iota(x.shape, 0)
    a = jnp.where(row < HD, x, 0.0)
    b = jnp.where((row >= HD) & (row < W), x, 0.0)
    return jnp.concatenate([a, b], axis=1).astype(BF16)


def pick(x2):
    n = x2.shape[0] // 2
    lane = iota((n, WP), 1)
    return jnp.where(lane < HD, x2[:n], x2[n:])


def each(n, f):
    lax.fori_loop(1, n, lambda i, c: (f(i), c)[1], 0)


class Exchange:
    def __init__(self, n, out, into):
        self.n, self.out, self.into = n, out, into

    def start(self):
        each(self.n, lambda i: self.out(i).start())

    def arrive(self):
        each(self.n, lambda i: self.into(i).wait_recv())

    def sent(self):
        each(self.n, lambda i: self.out(i).wait_send())


def kernel(
    q_hbm, k_hbm, v_hbm, w_hbm, go_hbm,
    lay_ref, gq_ref, gk_ref, gv_ref, gw_ref,
    xin, w_ref, go_ref, kv, q2, q2t, d2, d2t, acc2, m_ref, l_ref, gq2, own,
    part, mpin, cola, colain, colxin, cold, coldin, colo, coloin, coli, coliin,
    colg, colgin, colh, colhin, viax, viah,
    att, goh, goin, gwin, gz1, z1in, gz2, z2in, gfx, fxin, rbs, rbin, info, dat,
    in_s, row_s, row_r, rb_s, rb_r, mp_s, mp_r, ag_s, ag_r,
    ca_s, ca_r, cx_s, cx_r, cd_s, cd_r, co_s, co_r, ci_s, ci_r, cg_s, cg_r, ch_s, ch_r, hop_s, hop_r, vx_s, vh_s,
    go_s, go_r, gw_s, gw_r, z1_s, z1_r, z2_s, z2_r, fx_s, fx_r,
):
    s = lax.axis_index("seq")
    m = lax.axis_index("mp")
    cg = s % 8
    yh, x, z = s // 64, (s // 16) % 4, s % 16
    zq, zr = z // 4, z % 4
    g = yh * 4 + x

    def copy(src, dst, ss, rs, dev):
        return pltpu.make_async_remote_copy(
            src_ref=src, dst_ref=dst, send_sem=ss, recv_sem=rs, device_id=dev, device_id_type=MESH
        )

    def exchange(n, me, dev, src, dst, ss, rs):
        def other(i):
            return (me + i) % n

        def out(i):
            o = other(i)
            return copy(src(o), dst.at[me], ss.at[o], rs.at[me], dev(o))

        def into(i):
            o = other(i)
            return copy(src(o), dst.at[o], ss.at[o], rs.at[o], dev(o))

        return Exchange(n, out, into)

    def g_dev(o):
        return ((o // 4) * 64 + (o % 4) * 16 + z, m)

    def z_dev(o):
        return (yh * 64 + x * 16 + o, m)

    def mp_dev(o):
        return (s, o)

    def columns(src, dst, ss, rs):
        return exchange(8, g, g_dev, lambda o: src.at[o], dst, ss, rs)

    def far_dev(o, d):
        return ((o // 4) * 64 + (o % 4) * 16 + (z + 16 + d) % 16, m)

    class Across:
        def __init__(self, src, dst, via, d, ss, rs, vs, k):
            self.src, self.dst, self.via, self.d, self.ss, self.rs, self.vs, self.k = src, dst, via, d, ss, rs, vs, k

        def hop(self):
            return copy(self.src(pl.ds(4, 4)), self.via, hop_s.at[self.k], hop_r.at[self.k], far_dev(g, self.d))

        def straight(self, o):
            return copy(self.src(o), self.dst.at[g], self.ss.at[o], self.rs.at[g], far_dev(o, 8))

        def onward(self, o):
            return copy(self.via.at[o], self.dst.at[g], self.vs.at[o], self.rs.at[g], far_dev(o + 4, 7 * self.d))

        def start(self):
            self.hop().start()
            lax.fori_loop(0, 4, lambda o, c: (self.straight(o).start(), c)[1], 0)

        def relay(self):
            self.hop().wait_recv()
            lax.fori_loop(0, 4, lambda o, c: (self.onward(o).start(), c)[1], 0)

        def arrive(self):
            def one(o, c):
                copy(self.src(o), self.dst.at[o], self.ss.at[o], self.rs.at[o], far_dev(o, 8)).wait_recv()
                return c

            lax.fori_loop(0, 8, one, 0)

        def sent(self):
            def one(o, c):
                self.straight(o).wait_send()
                self.onward(o).wait_send()
                return c

            self.hop().wait_send()
            lax.fori_loop(0, 4, one, 0)

    ex_mp = exchange(4, m, mp_dev, lambda o: part.at[o], mpin, mp_s, mp_r)
    ex_ag = exchange(4, m, mp_dev, lambda o: att.at[m], att, ag_s, ag_r)
    ex_ca = columns(cola, colain, ca_s, ca_r)
    ex_cx = Across(lambda o: cola.at[o, pl.ds(16, 32)], colxin, viax, -1, cx_s, cx_r, vx_s, 0)
    ex_cd = columns(cold, coldin, cd_s, cd_r)
    ex_co = columns(colo, coloin, co_s, co_r)
    ex_ci = columns(coli, coliin, ci_s, ci_r)
    ex_cg = columns(colg, colgin, cg_s, cg_r)
    ex_ch = Across(lambda o: colh.at[o], colhin, viah, 1, ch_s, ch_r, vh_s, 1)
    ex_go = exchange(8, g, g_dev, lambda o: goh.at[o // 4], goin, go_s, go_r)
    ex_gw = exchange(8, g, g_dev, lambda o: att.at[o % 4], gwin, gw_s, gw_r)
    ex_z1 = exchange(4, zr, lambda o: z_dev(zq * 4 + o), lambda o: gz1.at[o], z1in, z1_s, z1_r)
    ex_z2 = exchange(4, zq, lambda o: z_dev(o * 4 + zr), lambda o: gz2.at[o], z2in, z2_s, z2_r)
    ex_fx = exchange(4, x, lambda o: (yh * 64 + o * 16 + z, m), lambda o: gfx.at[o], fxin, fx_s, fx_r)

    loads = [
        pltpu.make_async_copy(a, b, in_s.at[i])
        for i, (a, b) in enumerate(
            (
                (q_hbm, xin.at[0]), (k_hbm, xin.at[1]), (v_hbm, xin.at[2]),
                (go_hbm, go_ref), (w_hbm, w_ref),
            )
        )
    ]
    for c in loads:
        c.start()
    kv[:, :, 288:, :] = jnp.zeros((8, 2, WP - 288, TOK), BF16)
    bar = pltpu.get_barrier_semaphore()

    def greet(dev):
        pl.semaphore_signal(bar, inc=1, device_id=dev, device_id_type=MESH)

    each(8, lambda i: greet(g_dev((g + i) % 8)))

    def greet_sender(o, c):
        @pl.when(g < 4)
        def _():
            greet(far_dev(o, 8))

        @pl.when(g >= 4)
        def _():
            greet(far_dev(o, 7))
            greet(far_dev(o, -7))

        return c

    lax.fori_loop(0, 8, greet_sender, 0)
    greet(far_dev(g, 1))
    greet(far_dev(g, -1))
    each(4, lambda i: greet((s, (m + i) % 4)))
    each(4, lambda i: greet(z_dev(zq * 4 + (zr + i) % 4)))
    each(4, lambda i: greet(z_dev(((zq + i) % 4) * 4 + zr)))

    @pl.when(cg > 0)
    def _():
        greet((s - 1, m))

    @pl.when(cg < 7)
    def _():
        greet((s + 1, m))

    for c in loads[:3]:
        c.wait()
    kv[0, 0, :W, :] = xin[1]
    kv[0, 1, :W, :] = xin[2]
    fill = jnp.zeros((WP - W, TOK), F32)
    qt = jnp.concatenate([xin[0].astype(F32), fill], axis=0)
    q2t[...] = head_columns(qt)
    q32 = qt.T
    k32 = kv[0, 0].astype(F32).T
    v32 = kv[0, 1].astype(F32).T
    q2[...] = head_pair(q32)
    for i, t in enumerate((q32, k32, v32)):
        cola[:, 16 * i : 16 * i + 16, :] = t.astype(BF16).reshape(8, 16, WP)
    for c in loads[3:]:
        c.wait()
    pg = nt(go_ref[...], w_ref[...])
    lanes = jnp.zeros((TOK, WP - W), F32)
    for i in range(4):
        part[i] = jnp.concatenate([pg[:, W * i : W * i + W], lanes], axis=1).astype(BF16)
    go_t = go_ref[...].astype(F32).T.astype(BF16)
    goh[0] = go_t[:320]
    goh[1] = go_t[320:]

    links = (cg > 0).astype(jnp.int32) + (cg < 7).astype(jnp.int32)
    pl.semaphore_wait(bar, 7 + 4 + 8 + 2 + 3 + 3 + 3 + links)

    def row_copy(t, i):
        return copy(
            kv.at[t, i, pl.ds(0, WR)], kv.at[t + 1, i, pl.ds(0, WR)],
            row_s.at[t, i], row_r.at[t + 1, i], (s + 1, m),
        )

    def row_arrival(t, i):
        return copy(
            kv.at[t, i, pl.ds(0, WR)], kv.at[t, i, pl.ds(0, WR)],
            row_s.at[t, i], row_r.at[t, i], (s - 1, m),
        )

    @pl.when(cg < 7)
    def _():
        row_copy(0, 0).start()
        row_copy(0, 1).start()

    ex_cx.start()
    ex_mp.start()
    ex_ca.start()
    colain[g] = cola[g]
    ex_go.start()
    goin[g] = goh[yh]

    def scores(t):
        return nn(q2[...], kv[t, 0]) * SCALE

    def row_first():
        sc = scores(0)
        ok = iota((256, TOK), 0) % TOK >= iota((256, TOK), 1)
        sc = jnp.where(ok, sc, NEG)
        mx = jnp.max(sc, axis=1, keepdims=True)
        p = jnp.exp(sc - mx)
        m_ref[...] = mx
        l_ref[...] = jnp.sum(p, axis=1, keepdims=True)
        acc2[...] = nt(p.astype(BF16), kv[0, 1])

    def row_step(t):
        @pl.when(cg >= t)
        def _():
            for i in range(2):
                row_arrival(t, i).wait_recv()

                @pl.when(cg < 7)
                def _():
                    row_copy(t, i).start()

            sc = scores(t)
            old = m_ref[...]
            mx = jnp.maximum(old, jnp.max(sc, axis=1, keepdims=True))
            p = jnp.exp(sc - mx)
            w = jnp.exp(old - mx)
            m_ref[...] = mx
            l_ref[...] = l_ref[...] * w + jnp.sum(p, axis=1, keepdims=True)
            acc2[...] = acc2[...] * w + nt(p.astype(BF16), kv[t, 1])

    def row_steps(lo, hi):
        lax.fori_loop(lo, hi, lambda t, c: (row_step(t), c)[1], 0)

    def finish_dattn():
        ex_mp.arrive()
        d = part[m].astype(F32)
        for i in range(1, 4):
            d = d + mpin[(m + i) % 4].astype(F32)
        d = d.astype(BF16).astype(F32)
        dat[...] = d
        d2[...] = head_pair(d)
        d2t[...] = head_columns(d.T)
        cold[...] = d.astype(BF16).reshape(8, 16, WP)
        ex_cd.start()
        coldin[g] = cold[g]

    def column_rows(ref, i):
        return ref[:, 16 * i : 16 * i + 16, :].reshape(TOK, WP)

    def column_operands():
        ck = jnp.concatenate([column_rows(colain, 1), column_rows(colxin, 0)], axis=0)
        cv = jnp.concatenate([column_rows(colain, 2), column_rows(colxin, 1)], axis=0)
        return head_pair(column_rows(colain, 0).astype(F32)), ck, cv

    def column_mask(shape, qdim):
        qi = iota(shape, qdim) % TOK
        kj = iota(shape, 1 - qdim)
        ki = kj % TOK
        later = jnp.where(kj < TOK, 0, z // 8)
        return (qi % 16 == ki % 16) & (ki // 16 < qi // 16 + later)

    def col_forward():
        ex_ca.arrive()
        ex_cx.arrive()
        cq2, ck, cv = column_operands()
        sc = nt(cq2, ck) * SCALE
        ok = column_mask((256, 256), 0)
        mx = jnp.max(jnp.where(ok, sc, NEG), axis=1, keepdims=True)
        p = jnp.where(ok, jnp.exp(sc - mx), 0.0)
        tot = jnp.sum(p, axis=1, keepdims=True)
        some = tot > 0.0
        safe = jnp.where(some, tot, 1.0)
        o = pick(nn(p.astype(BF16), cv) / safe)
        lse = jnp.where(some, mx + jnp.log(safe), NEG)
        lane = iota((TOK, WP), 1)
        o = jnp.where(lane < W, o, jnp.where(lane < 340, lse[:TOK], lse[TOK:]))
        colo[...] = o.reshape(8, 16, WP)
        ex_co.start()
        coloin[g] = colo[g]

    def merge():
        ex_co.arrive()
        far = coloin[...].reshape(TOK, WP)
        lane = iota((TOK, WP), 1)
        d = dat[...]
        near = pick(acc2[...])
        lses, near_w, far_w = [], [], []
        for h in range(2):
            lo = W + 40 * h
            here = (lane >= lo) & (lane < lo + 40)
            fl = jnp.max(jnp.where(here, far, -3e38), axis=1, keepdims=True)
            mr = m_ref[h * TOK : h * TOK + TOK, :]
            nl = mr + jnp.log(l_ref[h * TOK : h * TOK + TOK, :])
            top = jnp.maximum(nl, fl)
            lse = top + jnp.log(jnp.exp(nl - top) + jnp.exp(fl - top))
            lses.append(lse)
            near_w.append(jnp.exp(mr - lse))
            far_w.append(jnp.exp(fl - lse))
        nw = jnp.where(lane < HD, near_w[0], near_w[1])
        fw = jnp.where(lane < HD, far_w[0], far_w[1])
        a = jnp.where(lane < W, near * nw + far * fw, 0.0).astype(BF16)
        att[m] = a
        ex_ag.start()
        prod = a.astype(F32) * d
        d0 = jnp.sum(jnp.where(lane < HD, prod, 0.0), axis=1, keepdims=True)
        d1 = jnp.sum(jnp.where((lane >= HD) & (lane < W), prod, 0.0), axis=1, keepdims=True)
        ln = iota((TOK, TOK), 1)
        both = jnp.where(ln < 64, jnp.where(ln < 32, lses[0], lses[1]), jnp.where(ln < 96, d0, d1))
        coli[...] = both.reshape(8, 16, TOK)
        ex_ci.start()
        coliin[g] = coli[g]
        info[...] = both
        gq2[...] = jnp.zeros_like(gq2)

    def stats(a):
        pair = [jnp.concatenate([a[:, i : i + 1], a[:, i + 32 : i + 33]], axis=0) for i in (0, 64)]
        return pair[0], pair[1]

    def row_own(u):
        @pl.when(cg >= u)
        def _():
            t = cg - u
            lse, delta = stats(info[...])
            k_t, v_t = kv[t, 0], kv[t, 1]
            ok = (t > 0) | (iota((256, TOK), 0) % TOK >= iota((256, TOK), 1))
            p = jnp.where(ok, jnp.exp(scores(t) - lse), 0.0)
            dp = nn(d2[...], v_t)
            ds = (p * (dp - delta)).astype(BF16)
            own[u, 0] = (nn(q2t[...], ds) * SCALE)[:WR]
            own[u, 1] = nn(d2t[...], p.astype(BF16))[:WR]
            gq2[...] += nt(ds, k_t)

    def rb_copy(u, i):
        return copy(rbs.at[u, i], rbin.at[u, i], rb_s.at[u, i], rb_r.at[u, i], (s - 1, m))

    def row_chain(u):
        @pl.when(cg >= u)
        def _():
            for i in range(2):
                @pl.when(cg < 7)
                def _():
                    rb_copy(u, i).wait_recv()
                    own[u, i] += rbin[u, i].astype(F32)

                @pl.when(cg > u)
                def _():
                    rbs[u, i] = own[u, i].astype(BF16)
                    rb_copy(u, i).start()

    def gather_attn():
        ex_ag.arrive()
        ex_gw.start()
        gwin[g] = att[x]

    def layer():
        full = jnp.concatenate([att[i].astype(F32)[:, :W] for i in range(4)], axis=1).astype(BF16)
        lay_ref[...] = nn(full, w_ref[...]).astype(BF16)

    def gw_product():
        ex_go.arrive()
        ex_gw.arrive()
        prod = nn(goin[0], gwin[0])
        for i in range(1, 8):
            prod = prod + nn(goin[i], gwin[i])
        to = iota((320, 320), 0)
        src = ((to // 5 % 4) * 16 + (to // 20 % 4) * 4 + to // 80) * 5 + to % 5
        perm = (src == iota((320, 320), 1)).astype(F32).astype(BF16)
        gz1[...] = nn(perm, prod.astype(BF16)).astype(BF16).reshape(4, 80, WP)
        ex_z1.start()

    def gw_level1():
        ex_z1.arrive()
        t = gz1[zr].astype(F32)
        for i in range(1, 4):
            t = t + z1in[(zr + i) % 4].astype(F32)
        to = iota((TOK, 80), 0)
        src = jnp.where(to % 8 < 5, to // 8 * 5 + to % 8, -1)
        perm = (src == iota((TOK, 80), 1)).astype(F32).astype(BF16)
        gz2[...] = nn(perm, t.astype(BF16)).astype(BF16).reshape(4, 32, WP)
        ex_z2.start()

    def gw_level2():
        ex_z2.arrive()
        t = gz2[zq].astype(F32)
        for i in range(1, 4):
            t = t + z2in[(zq + i) % 4].astype(F32)
        gfx[...] = t.reshape(4, 8, WP)
        ex_fx.start()
        fxin[x] = gfx[x]

    def gw_finish():
        ex_fx.arrive()
        gw_ref[...] = jnp.concatenate([fxin[i][:, :W] for i in range(4)], axis=1)[:5]

    def col_backward():
        ex_ci.arrive()
        ex_cd.arrive()
        cq2, ck, cv = column_operands()
        cd2 = head_pair(coldin[...].reshape(TOK, WP).astype(F32))
        both = coliin[...].reshape(TOK, TOK).T
        lse = jnp.concatenate([both[0:1], both[32:33]], axis=1)
        delta = jnp.concatenate([both[64:65], both[96:97]], axis=1)
        sc = nt(ck, cq2) * SCALE
        ok = column_mask((256, 256), 1)
        p = jnp.where(ok, jnp.exp(sc - lse), 0.0)
        dp = nt(cv, cd2)
        ds = (p * (dp - delta)).astype(BF16)
        ggk = nn(ds, cq2) * SCALE
        ggv = nn(p.astype(BF16), cd2)
        ggq = pick(tn(ds, ck)) * SCALE
        for i, t in enumerate((ggk, ggv)):
            colh[:, 16 * i : 16 * i + 16, :] = t[TOK:].astype(BF16).reshape(8, 16, WP)
        ex_ch.start()
        for i, t in enumerate((ggq, ggk[:TOK], ggv[:TOK])):
            colg[:, 16 * i : 16 * i + 16, :] = t.astype(BF16).reshape(8, 16, WP)
        ex_cg.start()
        colgin[g] = colg[g]

    def both(u):
        row_own(u)
        row_chain(u)

    def results():
        ex_cg.arrive()
        ex_ch.arrive()
        hq, hk, hv = (column_rows(colgin, i).astype(F32) for i in range(3))
        hk = hk + column_rows(colhin, 0).astype(F32)
        hv = hv + column_rows(colhin, 1).astype(F32)
        gq_ref[...] = (pick(gq2[...]) * SCALE + hq).T[:W].astype(BF16)
        gk_ref[...] = (own[cg, 0] + hk.T[:WR])[:W].astype(BF16)
        gv_ref[...] = (own[cg, 1] + hv.T[:WR])[:W].astype(BF16)

    def tick(u):
        row_own(u)

        @pl.when(u + cg >= 7)
        def _():
            row_chain(u + cg - 7)

    def ticks(lo, hi):
        lax.fori_loop(lo, hi, lambda u, c: (tick(u), c)[1], 0)

    row_first()
    ex_cx.relay()
    finish_dattn()
    row_steps(1, 3)
    col_forward()
    row_steps(3, 8)
    merge()
    gather_attn()
    ticks(0, 1)
    col_backward()
    ticks(1, 2)
    ex_ch.relay()
    gw_product()
    ticks(2, 5)
    gw_level1()
    ticks(5, 7)
    gw_level2()
    ticks(7, 8)
    layer()
    results()
    gw_finish()

    def sent(t, c):
        @pl.when((cg < 7) & (t <= cg))
        def _():
            row_copy(t, 0).wait_send()
            row_copy(t, 1).wait_send()

        @pl.when(t < cg)
        def _():
            rb_copy(t, 0).wait_send()
            rb_copy(t, 1).wait_send()

        return c

    lax.fori_loop(0, 8, sent, 0)
    for e in (ex_mp, ex_ag, ex_ca, ex_cx, ex_cd, ex_co, ex_ci, ex_cg, ex_ch, ex_go, ex_gw, ex_z1, ex_z2, ex_fx):
        e.sent()


def hand_over(*refs):
    for a, b in zip(refs[:5], refs[5:]):
        b[...] = a[...]


def body(queries, keys, values, weight_out, grad_out):
    vm = pl.BlockSpec(memory_space=pltpu.VMEM)
    hbm = pl.BlockSpec(memory_space=pltpu.HBM)
    dma = pltpu.SemaphoreType.DMA
    vmem = pltpu.VMEM
    out = jax.ShapeDtypeStruct
    scratch = [
        vmem((3, W, TOK), BF16),
        vmem((4 * W, 640), BF16),
        vmem((TOK, 640), BF16),
        vmem((8, 2, WP, TOK), BF16),
        vmem((256, WP), BF16),
        vmem((WP, 256), BF16),
        vmem((256, WP), BF16),
        vmem((WP, 256), BF16),
        vmem((256, WP), F32),
        vmem((256, 1), F32),
        vmem((256, 1), F32),
        vmem((256, WP), F32),
        vmem((8, 2, WR, TOK), F32),
        vmem((4, TOK, WP), BF16),
        vmem((4, TOK, WP), BF16),
        vmem((8, 48, WP), BF16),
        vmem((8, 48, WP), BF16),
        vmem((8, 32, WP), BF16),
        vmem((8, 16, WP), BF16),
        vmem((8, 16, WP), BF16),
        vmem((8, 16, WP), F32),
        vmem((8, 16, WP), F32),
        vmem((8, 16, TOK), F32),
        vmem((8, 16, TOK), F32),
        vmem((8, 48, WP), BF16),
        vmem((8, 48, WP), BF16),
        vmem((8, 32, WP), BF16),
        vmem((8, 32, WP), BF16),
        vmem((4, 32, WP), BF16),
        vmem((4, 32, WP), BF16),
        vmem((4, TOK, WP), BF16),
        vmem((2, 320, TOK), BF16),
        vmem((8, 320, TOK), BF16),
        vmem((8, TOK, WP), BF16),
        vmem((4, 80, WP), BF16),
        vmem((4, 80, WP), BF16),
        vmem((4, 32, WP), BF16),
        vmem((4, 32, WP), BF16),
        vmem((4, 8, WP), F32),
        vmem((4, 8, WP), F32),
        vmem((8, 2, WR, TOK), BF16),
        vmem((8, 2, WR, TOK), BF16),
        vmem((TOK, TOK), F32),
        vmem((TOK, WP), F32),
    ]
    sems = [dma((5,))] + [dma((8, 2))] * 4 + [dma((4,))] * 4 + [dma((8,))] * 14 + [dma((2,))] * 2 + [dma((4,))] * 2 + [dma((8,))] * 4 + [dma((4,))] * 6
    shapes = (
        out((TOK, 640), BF16),
        out((W, TOK), BF16),
        out((W, TOK), BF16),
        out((W, TOK), BF16),
        out((5, 4 * W), F32),
    )
    outs = pl.pallas_call(
        kernel,
        out_shape=shapes,
        in_specs=[hbm] * 5,
        out_specs=[vm] * 5,
        scratch_shapes=scratch + sems,
        compiler_params=pltpu.CompilerParams(
            collective_id=0, has_side_effects=True, vmem_limit_bytes=62 * 2**20
        ),
    )(queries.T, keys.T, values.T, weight_out.T, grad_out)
    lay, gq, gk, gv, gw = pl.pallas_call(
        hand_over, out_shape=shapes, in_specs=[vm] * 5, out_specs=[vm] * 5
    )(*outs)
    return lay, gq.T, gk.T, gv.T, gw


def solution(mesh):
    placed = (P("seq", "mp"), P("seq", "mp"), P("seq", "mp"), P("mp", None), P("seq", "mp"))
    return jax.shard_map(
        body,
        mesh=mesh,
        in_specs=placed,
        out_specs=(
            P("seq", "mp"),
            P("seq", "mp"),
            P("seq", "mp"),
            P("seq", "mp"),
            P(("mp", "seq"), None),
        ),
        check_vma=False,
    )
```

time: 172 us -> 133 us (0.77)
  the two profiles are of different devices: /device:TPU:24 before, /device:TPU:176 now
where the time goes in v2:
time: 133 us; the launch traced here: 132 us
  Pallas kernels  132 us (99%)
    pallas_call x1, Pallas kernels, body(): pl.pallas_call(kernel, out_shape=shapes, in_specs=[hbm] * 5, out_specs=[v...  130 us

profile of v2, /device:TPU:176, one launch (start us, length us, event | category | flops | bytes accessed | tf_op | source)
XLA Modules:
  0.0 132.4 jit_solution(1663822278879881200)
XLA Ops:
  0.6 130.0 %shard_map.92 = (bf16[128,640]{1,0:T(8,128)(2,1)}, bf16[300,128]{1,0:T(8,128)(2,1)}, bf16[300,128]{1,0:T(8,128)(2,1)}, bf16[300,128]{1,0:T(8,128)(2,1)}, f32[5,1200]{1,0:T(8,128)}) custom-call(bf16[300,128]{1,0:T(8,128)(2,1)} %bitcast.8, bf16[300,128]{1,0:T(8,128)(2,1)} %bitcast.9, bf16[300,128]{1,0:T(8,128)(2,1)} %bitcast.10, bf16[1200,640]{1,0:T(8,128)(2,1)} %bitcast.7, ...), custom_call_target="tpu_custom_call" | custom-call | tf_op jit(solution)/shard_map/pallas_call | solution.py:623
  130.6 1.8 %shard_map.93 = (bf16[128,640]{1,0:T(8,128)(2,1)}, bf16[300,128]{1,0:T(8,128)(2,1)}, bf16[300,128]{1,0:T(8,128)(2,1)}, bf16[300,128]{1,0:T(8,128)(2,1)}, f32[5,1200]{1,0:T(8,128)}) custom-call(bf16[128,640]{1,0:T(8,128)(2,1)} %get-tuple-element.15.refs_0_, bf16[300,128]{1,0:T(8,128)(2,1)} %get-tuple-element.16.refs_1_, ...), custom_call_target="tpu_custom_call" | custom-call | tf_op jit(solution)/shard_map/pallas_call | solution.py:633

commit v3 on v2

--- a/solution.py
+++ b/solution.py
@@ -7,6 +7,8 @@
 
 MESH = pl.DeviceIdType.MESH
 HD = 150
+VIA_OUT = 0
+VIA_BACK = 4
 W = 300
 WP = 384
 WR = 304
@@ -124,25 +126,28 @@
         return ((o // 4) * 64 + (o % 4) * 16 + (z + 16 + d) % 16, m)
 
     class Across:
-        def __init__(self, src, dst, via, d, ss, rs, vs, k):
+        def __init__(self, n, src, dst, via, d, ss, rs, vs, k):
+            self.n, self.first = n, 8 - n
             self.src, self.dst, self.via, self.d, self.ss, self.rs, self.vs, self.k = src, dst, via, d, ss, rs, vs, k
 
         def hop(self):
-            return copy(self.src(pl.ds(4, 4)), self.via, hop_s.at[self.k], hop_r.at[self.k], far_dev(g, self.d))
+            return copy(self.src(pl.ds(self.first, self.n)), self.via.at[pl.ds(0, self.n)], hop_s.at[self.k], hop_r.at[self.k], far_dev(g, self.d))
 
         def straight(self, o):
             return copy(self.src(o), self.dst.at[g], self.ss.at[o], self.rs.at[g], far_dev(o, 8))
 
         def onward(self, o):
-            return copy(self.via.at[o], self.dst.at[g], self.vs.at[o], self.rs.at[g], far_dev(o + 4, 7 * self.d))
+            return copy(self.via.at[o], self.dst.at[g], self.vs.at[o], self.rs.at[g], far_dev(o + self.first, 7 * self.d))
 
         def start(self):
-            self.hop().start()
-            lax.fori_loop(0, 4, lambda o, c: (self.straight(o).start(), c)[1], 0)
+            if self.n:
+                self.hop().start()
+            lax.fori_loop(0, self.first, lambda o, c: (self.straight(o).start(), c)[1], 0)
 
         def relay(self):
-            self.hop().wait_recv()
-            lax.fori_loop(0, 4, lambda o, c: (self.onward(o).start(), c)[1], 0)
+            if self.n:
+                self.hop().wait_recv()
+                lax.fori_loop(0, self.n, lambda o, c: (self.onward(o).start(), c)[1], 0)
 
         def arrive(self):
             def one(o, c):
@@ -152,25 +157,47 @@
             lax.fori_loop(0, 8, one, 0)
 
         def sent(self):
-            def one(o, c):
-                self.straight(o).wait_send()
-                self.onward(o).wait_send()
-                return c
-
-            self.hop().wait_send()
-            lax.fori_loop(0, 4, one, 0)
+            lax.fori_loop(0, self.first, lambda o, c: (self.straight(o).wait_send(), c)[1], 0)
+            if self.n:
+                self.hop().wait_send()
+                lax.fori_loop(0, self.n, lambda o, c: (self.onward(o).wait_send(), c)[1], 0)
 
     ex_mp = exchange(4, m, mp_dev, lambda o: part.at[o], mpin, mp_s, mp_r)
     ex_ag = exchange(4, m, mp_dev, lambda o: att.at[m], att, ag_s, ag_r)
     ex_ca = columns(cola, colain, ca_s, ca_r)
-    ex_cx = Across(lambda o: cola.at[o, pl.ds(16, 32)], colxin, viax, -1, cx_s, cx_r, vx_s, 0)
+    ex_cx = Across(VIA_OUT, lambda o: cola.at[o, pl.ds(16, 32)], colxin, viax, -1, cx_s, cx_r, vx_s, 0)
     ex_cd = columns(cold, coldin, cd_s, cd_r)
     ex_co = columns(colo, coloin, co_s, co_r)
     ex_ci = columns(coli, coliin, ci_s, ci_r)
     ex_cg = columns(colg, colgin, cg_s, cg_r)
-    ex_ch = Across(lambda o: colh.at[o], colhin, viah, 1, ch_s, ch_r, vh_s, 1)
+    ex_ch = Across(VIA_BACK, lambda o: colh.at[o], colhin, viah, 1, ch_s, ch_r, vh_s, 1)
     ex_go = exchange(8, g, g_dev, lambda o: goh.at[o // 4], goin, go_s, go_r)
-    ex_gw = exchange(8, g, g_dev, lambda o: att.at[o % 4], gwin, gw_s, gw_r)
+
+    def gw_target(j):
+        return ((j // 4) * 64 + (m + 4 - j % 4) % 4 * 16 + z, j % 4)
+
+    def gw_source(o):
+        return ((o // 4) * 64 + (o % 4) * 16 + z, (x + m) % 4)
+
+    def gw_mine(j):
+        return (x == 0) & (j // 4 == yh) & (j % 4 == m)
+
+    def gw_out(j):
+        return copy(att.at[m], gwin.at[g, pl.ds(0, WR)], gw_s.at[j], gw_r.at[g], gw_target(j))
+
+    def gw_into(o):
+        return copy(att.at[m], gwin.at[o, pl.ds(0, WR)], gw_s.at[o], gw_r.at[o], gw_source(o))
+
+    def over8(skip, f):
+        def one(i, c):
+            @pl.when(jnp.logical_not(skip(i)))
+            def _():
+                f(i)
+
+            return c
+
+        lax.fori_loop(0, 8, one, 0)
+
     ex_z1 = exchange(4, zr, lambda o: z_dev(zq * 4 + o), lambda o: gz1.at[o], z1in, z1_s, z1_r)
     ex_z2 = exchange(4, zq, lambda o: z_dev(o * 4 + zr), lambda o: gz2.at[o], z2in, z2_s, z2_r)
     ex_fx = exchange(4, x, lambda o: (yh * 64 + o * 16 + z, m), lambda o: gfx.at[o], fxin, fx_s, fx_r)
@@ -187,6 +214,7 @@
     for c in loads:
         c.start()
     kv[:, :, 288:, :] = jnp.zeros((8, 2, WP - 288, TOK), BF16)
+    gwin[:, WR:, :] = jnp.zeros((8, WP - WR, TOK), BF16)
     bar = pltpu.get_barrier_semaphore()
 
     def greet(dev):
@@ -194,21 +222,24 @@
 
     each(8, lambda i: greet(g_dev((g + i) % 8)))
 
+    straight = 8 - min(VIA_OUT, VIA_BACK)
+
     def greet_sender(o, c):
-        @pl.when(g < 4)
+        @pl.when(g < straight)
         def _():
             greet(far_dev(o, 8))
 
-        @pl.when(g >= 4)
-        def _():
-            greet(far_dev(o, 7))
-            greet(far_dev(o, -7))
+        for n, d in ((VIA_OUT, 7), (VIA_BACK, -7)):
+            @pl.when(g >= 8 - n)
+            def _(d=d):
+                greet(far_dev(o, d))
 
         return c
 
     lax.fori_loop(0, 8, greet_sender, 0)
     greet(far_dev(g, 1))
     greet(far_dev(g, -1))
+    over8(lambda o: (x == 0) & (o == g), lambda o: greet(gw_source(o)))
     each(4, lambda i: greet((s, (m + i) % 4)))
     each(4, lambda i: greet(z_dev(zq * 4 + (zr + i) % 4)))
     each(4, lambda i: greet(z_dev(((zq + i) % 4) * 4 + zr)))
@@ -245,7 +276,7 @@
     goh[1] = go_t[320:]
 
     links = (cg > 0).astype(jnp.int32) + (cg < 7).astype(jnp.int32)
-    pl.semaphore_wait(bar, 7 + 4 + 8 + 2 + 3 + 3 + 3 + links)
+    pl.semaphore_wait(bar, 7 + straight + VIA_OUT + VIA_BACK + 2 + 8 + 3 + 3 + 3 + links - (x == 0).astype(jnp.int32))
 
     def row_copy(t, i):
         return copy(
@@ -374,8 +405,13 @@
         nw = jnp.where(lane < HD, near_w[0], near_w[1])
         fw = jnp.where(lane < HD, far_w[0], far_w[1])
         a = jnp.where(lane < W, near * nw + far * fw, 0.0).astype(BF16)
-        att[m] = a
-        ex_ag.start()
+        att[m] = a.astype(F32).T[:WR].astype(BF16)
+        over8(gw_mine, lambda j: gw_out(j).start())
+
+        @pl.when(x == 0)
+        def _():
+            gwin[g, 0:WR] = att[m]
+
         prod = a.astype(F32) * d
         d0 = jnp.sum(jnp.where(lane < HD, prod, 0.0), axis=1, keepdims=True)
         d1 = jnp.sum(jnp.where((lane >= HD) & (lane < W), prod, 0.0), axis=1, keepdims=True)
@@ -384,6 +420,7 @@
         coli[...] = both.reshape(8, 16, TOK)
         ex_ci.start()
         coliin[g] = coli[g]
+        ex_ag.start()
         info[...] = both
         gq2[...] = jnp.zeros_like(gq2)
 
@@ -422,21 +459,17 @@
                     rbs[u, i] = own[u, i].astype(BF16)
                     rb_copy(u, i).start()
 
-    def gather_attn():
+    def layer():
         ex_ag.arrive()
-        ex_gw.start()
-        gwin[g] = att[x]
-
-    def layer():
-        full = jnp.concatenate([att[i].astype(F32)[:, :W] for i in range(4)], axis=1).astype(BF16)
+        full = jnp.concatenate([att[i].astype(F32).T[:, :W] for i in range(4)], axis=1).astype(BF16)
         lay_ref[...] = nn(full, w_ref[...]).astype(BF16)
 
     def gw_product():
         ex_go.arrive()
-        ex_gw.arrive()
-        prod = nn(goin[0], gwin[0])
+        over8(lambda o: (x == 0) & (o == g), lambda o: gw_into(o).wait_recv())
+        prod = nt(goin[0], gwin[0])
         for i in range(1, 8):
-            prod = prod + nn(goin[i], gwin[i])
+            prod = prod + nt(goin[i], gwin[i])
         to = iota((320, 320), 0)
         src = ((to // 5 % 4) * 16 + (to // 20 % 4) * 4 + to // 80) * 5 + to % 5
         perm = (src == iota((320, 320), 1)).astype(F32).astype(BF16)
@@ -465,7 +498,7 @@
 
     def gw_finish():
         ex_fx.arrive()
-        gw_ref[...] = jnp.concatenate([fxin[i][:, :W] for i in range(4)], axis=1)[:5]
+        gw_ref[...] = jnp.concatenate([fxin[(i + 4 - m) % 4][:, :W] for i in range(4)], axis=1)[:5]
 
     def col_backward():
         ex_ci.arrive()
@@ -522,18 +555,17 @@
     col_forward()
     row_steps(3, 8)
     merge()
-    gather_attn()
-    ticks(0, 1)
+    ticks(0, 2)
     col_backward()
-    ticks(1, 2)
+    ticks(2, 3)
+    gw_product()
     ex_ch.relay()
-    gw_product()
-    ticks(2, 5)
+    ticks(3, 5)
     gw_level1()
     ticks(5, 7)
+    layer()
     gw_level2()
     ticks(7, 8)
-    layer()
     results()
     gw_finish()
 
@@ -551,8 +583,9 @@
         return c
 
     lax.fori_loop(0, 8, sent, 0)
-    for e in (ex_mp, ex_ag, ex_ca, ex_cx, ex_cd, ex_co, ex_ci, ex_cg, ex_ch, ex_go, ex_gw, ex_z1, ex_z2, ex_fx):
+    for e in (ex_mp, ex_ag, ex_ca, ex_cx, ex_cd, ex_co, ex_ci, ex_cg, ex_ch, ex_go, ex_z1, ex_z2, ex_fx):
         e.sent()
+    over8(gw_mine, lambda j: gw_out(j).wait_send())
 
 
 def hand_over(*refs):
@@ -595,12 +628,12 @@
         vmem((8, 48, WP), BF16),
         vmem((8, 32, WP), BF16),
         vmem((8, 32, WP), BF16),
-        vmem((4, 32, WP), BF16),
-        vmem((4, 32, WP), BF16),
-        vmem((4, TOK, WP), BF16),
+        vmem((8, 32, WP), BF16),
+        vmem((8, 32, WP), BF16),
+        vmem((4, WR, TOK), BF16),
         vmem((2, 320, TOK), BF16),
         vmem((8, 320, TOK), BF16),
-        vmem((8, TOK, WP), BF16),
+        vmem((8, WP, TOK), BF16),
         vmem((4, 80, WP), BF16),
         vmem((4, 80, WP), BF16),
         vmem((4, 32, WP), BF16),
@@ -612,7 +645,7 @@
         vmem((TOK, TOK), F32),
         vmem((TOK, WP), F32),
     ]
-    sems = [dma((5,))] + [dma((8, 2))] * 4 + [dma((4,))] * 4 + [dma((8,))] * 14 + [dma((2,))] * 2 + [dma((4,))] * 2 + [dma((8,))] * 4 + [dma((4,))] * 6
+    sems = [dma((5,))] + [dma((8, 2))] * 4 + [dma((4,))] * 4 + [dma((8,))] * 14 + [dma((2,))] * 2 + [dma((8,))] * 6 + [dma((4,))] * 6
     shapes = (
         out((TOK, 640), BF16),
         out((W, TOK), BF16),

time: 133 us -> 116 us (0.87)
  the two profiles are of different devices: /device:TPU:176 before, /device:TPU:104 now
where the time goes in v3:
time: 116 us
  Pallas kernels  116 us (100%)
    pallas_call x1, Pallas kernels, body(): pl.pallas_call(kernel, out_shape=shapes, in_specs=[hbm] * 5, out_specs=[v...  114 us

profile of v3, /device:TPU:104, one launch (start us, length us, event | category | flops | bytes accessed | tf_op | source)
XLA Modules:
  0.0 116.2 jit_solution(821614755875439006)
XLA Ops:
  0.6 113.7 %shard_map.92 = (bf16[128,640]{1,0:T(8,128)(2,1)}, bf16[300,128]{1,0:T(8,128)(2,1)}, bf16[300,128]{1,0:T(8,128)(2,1)}, bf16[300,128]{1,0:T(8,128)(2,1)}, f32[5,1200]{1,0:T(8,128)}) custom-call(bf16[300,128]{1,0:T(8,128)(2,1)} %bitcast.8, bf16[300,128]{1,0:T(8,128)(2,1)} %bitcast.9, bf16[300,128]{1,0:T(8,128)(2,1)} %bitcast.10, bf16[1200,640]{1,0:T(8,128)(2,1)} %bitcast.7, ...), custom_call_target="tpu_custom_call" | custom-call | tf_op jit(solution)/shard_map/pallas_call | solution.py:656
  114.4 1.8 %shard_map.93 = (bf16[128,640]{1,0:T(8,128)(2,1)}, bf16[300,128]{1,0:T(8,128)(2,1)}, bf16[300,128]{1,0:T(8,128)(2,1)}, bf16[300,128]{1,0:T(8,128)(2,1)}, f32[5,1200]{1,0:T(8,128)}) custom-call(bf16[128,640]{1,0:T(8,128)(2,1)} %get-tuple-element.15.refs_0_, bf16[300,128]{1,0:T(8,128)(2,1)} %get-tuple-element.16.refs_1_, ...), custom_call_target="tpu_custom_call" | custom-call | tf_op jit(solution)/shard_map/pallas_call | solution.py:666

commit v4 on v3

--- a/solution.py
+++ b/solution.py
@@ -7,7 +7,7 @@
 
 MESH = pl.DeviceIdType.MESH
 HD = 150
-VIA_OUT = 0
+VIA_OUT = 1
 VIA_BACK = 4
 W = 300
 WP = 384
@@ -55,6 +55,20 @@
     return jnp.where(lane < HD, x2[:n], x2[n:])
 
 
+def two_in_one(a, b):
+    rest = a[:, 256:] + pltpu.roll(b[:, 256:], 64, 1)
+    return jnp.concatenate([a[:, :256], b[:, :256], rest], axis=1).astype(BF16)
+
+
+def one_in_two(x):
+    x = x.astype(F32)
+    rest = x[:, 512:]
+    low = iota(rest.shape, 1) < 64
+    a = jnp.concatenate([x[:, :256], jnp.where(low, rest, 0.0)], axis=1)
+    b = jnp.concatenate([x[:, 256:512], jnp.where(low, pltpu.roll(rest, 64, 1), 0.0)], axis=1)
+    return a, b
+
+
 def each(n, f):
     lax.fori_loop(1, n, lambda i, c: (f(i), c)[1], 0)
 
@@ -77,7 +91,7 @@
     q_hbm, k_hbm, v_hbm, w_hbm, go_hbm,
     lay_ref, gq_ref, gk_ref, gv_ref, gw_ref,
     xin, w_ref, go_ref, kv, q2, q2t, d2, d2t, acc2, m_ref, l_ref, gq2, own,
-    part, mpin, cola, colain, colxin, cold, coldin, colo, coloin, coli, coliin,
+    part, mpin, cola, colain, colx, colxin, cold, coldin, colo, coloin, coli, coliin,
     colg, colgin, colh, colhin, viax, viah,
     att, goh, goin, gwin, gz1, z1in, gz2, z2in, gfx, fxin, rbs, rbin, info, dat,
     in_s, row_s, row_r, rb_s, rb_r, mp_s, mp_r, ag_s, ag_r,
@@ -165,7 +179,7 @@
     ex_mp = exchange(4, m, mp_dev, lambda o: part.at[o], mpin, mp_s, mp_r)
     ex_ag = exchange(4, m, mp_dev, lambda o: att.at[m], att, ag_s, ag_r)
     ex_ca = columns(cola, colain, ca_s, ca_r)
-    ex_cx = Across(VIA_OUT, lambda o: cola.at[o, pl.ds(16, 32)], colxin, viax, -1, cx_s, cx_r, vx_s, 0)
+    ex_cx = Across(VIA_OUT, lambda o: colx.at[o], colxin, viax, -1, cx_s, cx_r, vx_s, 0)
     ex_cd = columns(cold, coldin, cd_s, cd_r)
     ex_co = columns(colo, coloin, co_s, co_r)
     ex_ci = columns(coli, coliin, ci_s, ci_r)
@@ -265,6 +279,7 @@
     q2[...] = head_pair(q32)
     for i, t in enumerate((q32, k32, v32)):
         cola[:, 16 * i : 16 * i + 16, :] = t.astype(BF16).reshape(8, 16, WP)
+    colx[...] = two_in_one(k32, v32).reshape(8, 16, 640)
     for c in loads[3:]:
         c.wait()
     pg = nt(go_ref[...], w_ref[...])
@@ -299,8 +314,6 @@
     ex_mp.start()
     ex_ca.start()
     colain[g] = cola[g]
-    ex_go.start()
-    goin[g] = goh[yh]
 
     def scores(t):
         return nn(q2[...], kv[t, 0]) * SCALE
@@ -354,8 +367,9 @@
         return ref[:, 16 * i : 16 * i + 16, :].reshape(TOK, WP)
 
     def column_operands():
-        ck = jnp.concatenate([column_rows(colain, 1), column_rows(colxin, 0)], axis=0)
-        cv = jnp.concatenate([column_rows(colain, 2), column_rows(colxin, 1)], axis=0)
+        fk, fv = one_in_two(colxin[...].reshape(TOK, 640))
+        ck = jnp.concatenate([column_rows(colain, 1), fk.astype(BF16)], axis=0)
+        cv = jnp.concatenate([column_rows(colain, 2), fv.astype(BF16)], axis=0)
         return head_pair(column_rows(colain, 0).astype(F32)), ck, cv
 
     def column_mask(shape, qdim):
@@ -516,8 +530,7 @@
         ggk = nn(ds, cq2) * SCALE
         ggv = nn(p.astype(BF16), cd2)
         ggq = pick(tn(ds, ck)) * SCALE
-        for i, t in enumerate((ggk, ggv)):
-            colh[:, 16 * i : 16 * i + 16, :] = t[TOK:].astype(BF16).reshape(8, 16, WP)
+        colh[...] = two_in_one(ggk[TOK:], ggv[TOK:]).reshape(8, 16, 640)
         ex_ch.start()
         for i, t in enumerate((ggq, ggk[:TOK], ggv[:TOK])):
             colg[:, 16 * i : 16 * i + 16, :] = t.astype(BF16).reshape(8, 16, WP)
@@ -532,8 +545,9 @@
         ex_cg.arrive()
         ex_ch.arrive()
         hq, hk, hv = (column_rows(colgin, i).astype(F32) for i in range(3))
-        hk = hk + column_rows(colhin, 0).astype(F32)
-        hv = hv + column_rows(colhin, 1).astype(F32)
+        fk, fv = one_in_two(colhin[...].reshape(TOK, 640))
+        hk = hk + fk
+        hv = hv + fv
         gq_ref[...] = (pick(gq2[...]) * SCALE + hq).T[:W].astype(BF16)
         gk_ref[...] = (own[cg, 0] + hk.T[:WR])[:W].astype(BF16)
         gv_ref[...] = (own[cg, 1] + hv.T[:WR])[:W].astype(BF16)
@@ -551,9 +565,11 @@
     row_first()
     ex_cx.relay()
     finish_dattn()
-    row_steps(1, 3)
+    ex_go.start()
+    goin[g] = goh[yh]
+    row_steps(1, 4)
     col_forward()
-    row_steps(3, 8)
+    row_steps(4, 8)
     merge()
     ticks(0, 2)
     col_backward()
@@ -617,7 +633,8 @@
         vmem((4, TOK, WP), BF16),
         vmem((8, 48, WP), BF16),
         vmem((8, 48, WP), BF16),
-        vmem((8, 32, WP), BF16),
+        vmem((8, 16, 640), BF16),
+        vmem((8, 16, 640), BF16),
         vmem((8, 16, WP), BF16),
         vmem((8, 16, WP), BF16),
         vmem((8, 16, WP), F32),
@@ -626,10 +643,10 @@
         vmem((8, 16, TOK), F32),
         vmem((8, 48, WP), BF16),
         vmem((8, 48, WP), BF16),
-        vmem((8, 32, WP), BF16),
-        vmem((8, 32, WP), BF16),
-        vmem((8, 32, WP), BF16),
-        vmem((8, 32, WP), BF16),
+        vmem((8, 16, 640), BF16),
+        vmem((8, 16, 640), BF16),
+        vmem((8, 16, 640), BF16),
+        vmem((8, 16, 640), BF16),
         vmem((4, WR, TOK), BF16),
         vmem((2, 320, TOK), BF16),
         vmem((8, 320, TOK), BF16),

time: 116 us -> 108 us (0.931)
  the two profiles are of different devices: /device:TPU:104 before, /device:TPU:64 now
where the time goes in v4:
time: 108 us
  Pallas kernels  107 us (99%)
    pallas_call x1, Pallas kernels, body(): pl.pallas_call(kernel, out_shape=shapes, in_specs=[hbm] * 5, out_specs=[v...  105 us

profile of v4, /device:TPU:64, one launch (start us, length us, event | category | flops | bytes accessed | tf_op | source)
XLA Modules:
  0.0 107.6 jit_solution(5275672907129752645)
XLA Ops:
  0.6 105.1 %shard_map.92 = (bf16[128,640]{1,0:T(8,128)(2,1)}, bf16[300,128]{1,0:T(8,128)(2,1)}, bf16[300,128]{1,0:T(8,128)(2,1)}, bf16[300,128]{1,0:T(8,128)(2,1)}, f32[5,1200]{1,0:T(8,128)}) custom-call(bf16[300,128]{1,0:T(8,128)(2,1)} %bitcast.8, bf16[300,128]{1,0:T(8,128)(2,1)} %bitcast.9, bf16[300,128]{1,0:T(8,128)(2,1)} %bitcast.10, bf16[1200,640]{1,0:T(8,128)(2,1)} %bitcast.7, ...), custom_call_target="tpu_custom_call" | custom-call | tf_op jit(solution)/shard_map/pallas_call | solution.py:673
  105.8 1.8 %shard_map.93 = (bf16[128,640]{1,0:T(8,128)(2,1)}, bf16[300,128]{1,0:T(8,128)(2,1)}, bf16[300,128]{1,0:T(8,128)(2,1)}, bf16[300,128]{1,0:T(8,128)(2,1)}, f32[5,1200]{1,0:T(8,128)}) custom-call(bf16[128,640]{1,0:T(8,128)(2,1)} %get-tuple-element.15.refs_0_, bf16[300,128]{1,0:T(8,128)(2,1)} %get-tuple-element.16.refs_1_, ...), custom_call_target="tpu_custom_call" | custom-call | tf_op jit(solution)/shard_map/pallas_call | solution.py:683

commit v5 on v4

--- a/solution.py
+++ b/solution.py
@@ -8,7 +8,7 @@
 MESH = pl.DeviceIdType.MESH
 HD = 150
 VIA_OUT = 1
-VIA_BACK = 4
+VIA_BACK = 5
 W = 300
 WP = 384
 WR = 304

time: 108 us -> 107 us (level)
  the two profiles are of different devices: /device:TPU:64 before, /device:TPU:24 now
where the time goes in v5:
time: 107 us; the launch traced here: 106 us
  Pallas kernels  106 us (99%)
    pallas_call x1, Pallas kernels, body(): pl.pallas_call(kernel, out_shape=shapes, in_specs=[hbm] * 5, out_specs=[v...  104 us

profile of v5, /device:TPU:24, one launch (start us, length us, event | category | flops | bytes accessed | tf_op | source)
XLA Modules:
  0.0 106.5 jit_solution(17222776413935953881)
XLA Ops:
  0.6 104.0 %shard_map.92 = (bf16[128,640]{1,0:T(8,128)(2,1)}, bf16[300,128]{1,0:T(8,128)(2,1)}, bf16[300,128]{1,0:T(8,128)(2,1)}, bf16[300,128]{1,0:T(8,128)(2,1)}, f32[5,1200]{1,0:T(8,128)}) custom-call(bf16[300,128]{1,0:T(8,128)(2,1)} %bitcast.8, bf16[300,128]{1,0:T(8,128)(2,1)} %bitcast.9, bf16[300,128]{1,0:T(8,128)(2,1)} %bitcast.10, bf16[1200,640]{1,0:T(8,128)(2,1)} %bitcast.7, ...), custom_call_target="tpu_custom_call" | custom-call | tf_op jit(solution)/shard_map/pallas_call | solution.py:673
  104.7 1.8 %shard_map.93 = (bf16[128,640]{1,0:T(8,128)(2,1)}, bf16[300,128]{1,0:T(8,128)(2,1)}, bf16[300,128]{1,0:T(8,128)(2,1)}, bf16[300,128]{1,0:T(8,128)(2,1)}, f32[5,1200]{1,0:T(8,128)}) custom-call(bf16[128,640]{1,0:T(8,128)(2,1)} %get-tuple-element.15.refs_0_, bf16[300,128]{1,0:T(8,128)(2,1)} %get-tuple-element.16.refs_1_, ...), custom_call_target="tpu_custom_call" | custom-call | tf_op jit(solution)/shard_map/pallas_call | solution.py:683
